TPU v7x, 512 devices: a whole 4x4x16 slice. The times are simulated.
512 devices in a mesh: seq: 16 (over y, x_hi, core), exp: 32 (over z, x_lo).
Axes of the slice: x: 4 (x_hi: 2, x_lo: 2; x = x_hi * 2 + x_lo), y: 4, z: 16, core: 2. Of those that a mesh axis runs over, the one named last changes fastest.
Arguments:
- queries: bfloat16 [2048, 4096], P('seq', 'exp'), may hold values from -6 to 6
- key_states: bfloat16 [2048, 512], P('seq'), may hold values from -6 to 6
- value_states: bfloat16 [2048, 512], P('seq'), may hold values from -6 to 6
- residual: bfloat16 [2048, 4096], P('seq', 'exp'), may hold values from -54 to 54
- out_proj: bfloat16 [4096, 4096], P('exp'), may hold values from -0.5 to 0.5
- norm_gain: float32 [4096], replicated, may hold values from 0.1 to 1.9
- expert_ids: int32 [2048, 8], P('seq'), may hold values from 0 to 63, all different within a row; in each aligned block of 128 rows (0 to 127, 128 to 255, ...) at most 32 rows name the same one
- gate_scores: float32 [2048, 8], P('seq'), may hold values from 0.05 to 1
- w_gate: bfloat16 [64, 1024, 4096], P('exp', 'seq'), may hold values from -0.09375 to 0.09375
- w_up: bfloat16 [64, 1024, 4096], P('exp', 'seq'), may hold values from -0.09375 to 0.09375
- w_down: bfloat16 [64, 1024, 4096], P('exp', None, 'seq'), may hold values from -0.375 to 0.375
Outputs:
- attn_out: bfloat16 [2048, 4096], P('seq', 'exp')
- expert_out: bfloat16 [2048, 4096], P('seq', 'exp')
Inputs may be any that keep to these rules, and one draw needn't show every extreme that they name: `expert_ids`: each row names 8 different experts. In each aligned block of 128 rows no expert is named by more than 32 rows, and in some block an expert is named by exactly 32 rows.
All inputs are finite; a program needn't handle non-finite values.
Results may differ from a plain program's by a relative error of at most 0.02.
Values may be sent and summed in bfloat16 or wider, within the bound.
A program may use at most 64 MiB of HBM per device.

v0:
```python
import jax
import jax.numpy as jnp
from jax import lax
from jax.sharding import PartitionSpec as P

HD = 128
KVH = 4
TOP = 8


NEG_FILL = -1e30
NORM_EPS = 1e-06


def tile_scores(query_rows, key_rows, value_rows, visible):
    scores = jnp.einsum(
        "qd,kd->qk", query_rows, key_rows, preferred_element_type=jnp.float32
    ) * HD ** (-0.5)
    scores = jnp.where(visible, scores, NEG_FILL)
    row_max = jnp.max(scores, axis=1)
    exp_weights = jnp.where(visible, jnp.exp(scores - row_max[:, None]), 0.0)
    row_total = jnp.sum(exp_weights, axis=1)
    weighted = jnp.dot(
        exp_weights.astype(jnp.bfloat16), value_rows, preferred_element_type=jnp.float32
    )
    return (row_max, row_total, weighted)


def merge_state(first_state, second_state):
    left_max, left_total, left_sum = first_state
    right_max, right_total, right_sum = second_state
    joint_max = jnp.maximum(left_max, right_max)
    right_scale = jnp.exp(right_max - joint_max)
    joint_total = right_total * right_scale
    joint_sum = right_sum * right_scale[:, None]
    return (joint_max, joint_total, joint_sum)


def slot_table(expert_ids, expert_list, capacity):
    row_count = expert_ids.shape[0]
    matches = expert_ids[:, None, :] == expert_list[None, :, None]
    is_routed = jnp.any(matches, axis=2).astype(jnp.float32)
    earlier_rows = (jnp.arange(row_count)[:, None] > jnp.arange(row_count)[None, :]).astype(
        jnp.float32
    )
    slot_rank = jnp.dot(earlier_rows, is_routed, precision=lax.Precision.HIGHEST)
    slot_index = jnp.arange(capacity, dtype=jnp.float32)
    return is_routed.T[:, None, :] * (slot_rank.T[:, None, :] == slot_index[None, :, None])


def per_device(
    queries,
    key_states,
    value_states,
    residual,
    out_proj,
    norm_gain,
    expert_ids,
    gate_scores,
    w_gate,
    w_up,
    w_down,
):
    row_count = queries.shape[0]
    seq_index = lax.axis_index("seq")
    exp_index = lax.axis_index("exp")
    exp_count = lax.axis_size("exp")
    group_size = exp_count // KVH
    kv_start = exp_index // group_size * HD
    head_keys = lax.dynamic_slice_in_dim(key_states, kv_start, HD, 1)
    head_values = lax.dynamic_slice_in_dim(value_states, kv_start, HD, 1)
    first_row = seq_index * row_count
    query_pos = first_row + jnp.arange(row_count)
    start_state = (
        jnp.full((row_count,), NEG_FILL, jnp.float32),
        jnp.zeros((row_count,), jnp.float32),
        jnp.zeros((row_count, HD), jnp.float32),
    )
    piece_keys = lax.all_gather(head_keys, "seq", axis=0, tiled=True)
    piece_values = lax.all_gather(head_values, "seq", axis=0, tiled=True)
    key_pos = jnp.arange(piece_keys.shape[0])

    def compute(carried):
        visible = query_pos[:, None] >= key_pos[None, :]
        return merge_state(carried, tile_scores(queries, piece_keys, piece_values, visible))

    attn_state = lax.cond(
        jnp.int32(0) < first_row + row_count, compute, lambda carried: carried, start_state
    )
    row_max, row_total, weighted = attn_state
    head_out = (weighted / row_total[:, None]).astype(jnp.bfloat16)
    partial_value = jnp.dot(head_out, out_proj, preferred_element_type=jnp.float32)
    col_width = residual.shape[1]
    first_col = exp_index * col_width
    residual_cols = residual.astype(jnp.float32)
    experts_here = w_gate.shape[0]
    capacity = 2 * row_count * TOP // (experts_here * exp_count)
    owned_ids = exp_index * experts_here + jnp.arange(experts_here)
    route_weight = gate_scores / jnp.sum(gate_scores, axis=1, keepdims=True)
    owned_matches = expert_ids[:, None, :] == owned_ids[None, :, None]
    route_share = jnp.sum(jnp.where(owned_matches, route_weight[:, None, :], 0.0), axis=2)
    current = lax.dynamic_slice_in_dim(partial_value, first_col, col_width, 1) + residual_cols
    partial_value = lax.dynamic_update_slice_in_dim(partial_value, current, first_col, 1)
    residual_sum = lax.psum(partial_value, "exp")
    mean_square = jnp.mean(residual_sum * residual_sum, axis=1, keepdims=True)
    normed = (residual_sum * lax.rsqrt(mean_square + NORM_EPS) * norm_gain).astype(jnp.bfloat16)
    summed_cols = lax.dynamic_slice_in_dim(residual_sum, first_col, col_width, 1)
    attn_cols = summed_cols - residual_cols
    picked = slot_table(expert_ids, owned_ids, capacity)
    chosen = jnp.einsum(
        "ecr,rd->ecd", picked.astype(jnp.bfloat16), normed, preferred_element_type=jnp.float32
    ).astype(jnp.bfloat16)
    segment = lax.all_gather(chosen[None], "seq", axis=0, tiled=True)
    gate_value = jnp.einsum("secd,efd->secf", segment, w_gate, preferred_element_type=jnp.float32)
    up_value = jnp.einsum("secd,efd->secf", segment, w_up, preferred_element_type=jnp.float32)
    hidden = (jax.nn.silu(gate_value) * up_value).astype(jnp.bfloat16)
    produced = jnp.einsum(
        "secf,efd->secd",
        lax.all_gather(hidden, "seq", axis=3, tiled=True),
        w_down,
        preferred_element_type=jnp.float32,
    )
    returned = lax.all_to_all(
        produced.astype(jnp.bfloat16), "seq", split_axis=0, concat_axis=3, tiled=True
    )
    placed_rows = jnp.einsum(
        "ecr,ecd->erd", picked.astype(jnp.bfloat16), returned[0], preferred_element_type=jnp.float32
    )
    expert_sum = jnp.sum(placed_rows * route_share.T[:, :, None], axis=0)
    expert_cols = lax.psum_scatter(expert_sum, "exp", scatter_dimension=1, tiled=True)
    return (attn_cols.astype(jnp.bfloat16), expert_cols.astype(jnp.bfloat16))


def solution(mesh):
    placed = (
        P("seq", "exp"),
        P("seq", None),
        P("seq", None),
        P("seq", "exp"),
        P("exp", None),
        P(),
        P("seq", None),
        P("seq", None),
        P("exp", "seq", None),
        P("exp", "seq", None),
        P("exp", None, "seq"),
    )
    return jax.shard_map(
        per_device,
        mesh=mesh,
        in_specs=placed,
        out_specs=(P("seq", "exp"), P("seq", "exp")),
        check_vma=False,
    )
```

profile of v0, /device:TPU:24, one launch (start us, length us, event | category | flops | bytes accessed | tf_op | source)
XLA Modules:
  0.0 690.4 jit_solution(18114156533302371187)
XLA Ops:
  7.2 0.8 constant_dynamic-slice_fusion.1
  8.1 0.8 constant_dynamic-slice_fusion
  8.8 24.3 %all_gather.13 = bf16[2048,128]{1,0:T(8,128)(2,1)S(1)} all-gather(bf16[128,128]{1,0:T(8,128)(2,1)S(1)} %constant_dynamic-slice_fusion), channel_id=1, replica_groups=mesh['seq'=16,'exp'=32] {'seq'}, dimensions={0}, use_global_device_ids=true | all-gather | bytes 557056 | tf_op jit(solution)/shard_map/all_gather | solution.py:80
  33.1 23.8 %all_gather.12 = bf16[2048,128]{1,0:T(8,128)(2,1)S(1)} all-gather(bf16[128,128]{1,0:T(8,128)(2,1)S(1)} %constant_dynamic-slice_fusion.1), channel_id=1, replica_groups=mesh['seq'=16,'exp'=32] {'seq'}, dimensions={0}, use_global_device_ids=true | all-gather | bytes 557056 | tf_op jit(solution)/shard_map/all_gather | solution.py:79
  56.9 1.9 conditional.1
  56.9 1.1 fusion.57
  58.9 0.5 fusion.46
  59.4 1.3 copy-done.1
  61.1 272.4 %all-reduce.2.cloned.1.call-done = f32[128,4096]{1,0:T(8,128)} async-done(((f32[128,4096]{1,0:T(8,128)}), f32[128,4096]{1,0:T(8,128)}) %all-reduce.2.cloned.1.call-update) | async-done | bytes 2097168 | tf_op jit(solution)/shard_map/psum | solution.py:104
  333.5 1.8 multiply_reduce_fusion
  335.3 2.8 convolution_convert_fusion
  338.2 84.7 %all-gather.6.cloned.1.call-done = bf16[32,32,4096]{2,1,0:T(8,128)(2,1)} async-done(((bf16[2,32,4096]{2,1,0:T(8,128)(2,1)}), bf16[32,32,4096]{2,1,0:T(8,128)(2,1)}) %all-gather.6.cloned.1.call-update) | async-done | bytes 8388624 | tf_op jit(solution)/shard_map/all_gather | solution.py:113
  423.0 5.8 fusion.24
  429.0 2.3 fusion.33
  431.3 1.5 copy.37
  432.9 86.4 %all-gather.4.cloned.1.call-done = bf16[16,2,32,1024]{2,0,1,3:T(8,128)(2,1)} async-done(((bf16[16,2,32,64]{2,0,1,3:T(8,128)(2,1)}), bf16[16,2,32,1024]{2,0,1,3:T(8,128)(2,1)}) %all-gather.4.cloned.1.call-update) | async-done | bytes 2097168 | tf_op jit(solution)/shard_map/all_gather | solution.py:119
  519.2 6.2 fusion.21
  525.4 0.8 copy.39
  526.3 5.8 all-to-all-start
  532.3 9.9 %all-to-all-done = bf16[16,2,32,256]{3,2,1,0:T(8,128)(2,1)S(1)} async-done(((bf16[16,2,32,256]{3,2,1,0:T(8,128)(2,1)}), bf16[16,2,32,256]{3,2,1,0:T(8,128)(2,1)S(1)}, u32[]{:S(2)}, u32[]{:S(2)}) %all-to-all-start) | async-done | bytes 524320 | tf_op jit(solution)/shard_map/all_to_all | solution.py:123
  542.7 2.1 fusion.17
  544.9 1.5 fusion.44
  546.3 136.1 %reduce-scatter.2.cloned.1.call-done = f32[128,128]{1,0:T(8,128)} async-done(((f32[128,4096]{1,0:T(8,128)}), f32[128,128]{1,0:T(8,128)}) %reduce-scatter.2.cloned.1.call-update) | async-done | bytes 65552 | tf_op jit(solution)/shard_map/reduce_scatter | solution.py:130
  682.4 1.5 convert_element_type.58
  (44 shorter events, 2.1 us)
Async XLA Ops:
  7.2 51.7 %copy-start = (bf16[128,4096]{1,0:T(8,128)(2,1)S(1)}, bf16[128,4096]{1,0:T(8,128)(2,1)}, u32[]{:S(2)}) copy-start(bf16[128,4096]{1,0:T(8,128)(2,1)} %param.17) | copy-start | bytes 3145732
  7.2 326.3 %all-reduce.2.cloned.1.call-start = ((), (), s32[]{:S(2)}) async-start(), calls=%async_computation.2 | async-start | bytes 4194304 | tf_op jit(solution)/shard_map/psum | solution.py:104
  33.1 26.2 %copy-start.3 = (bf16[128,128]{1,0:T(8,128)(2,1)S(1)}, bf16[128,128]{1,0:T(8,128)(2,1)}, u32[]{:S(2)}) copy-start(bf16[128,128]{1,0:T(8,128)(2,1)} %param.16) | copy-start | bytes 98308
  56.9 3.9 copy-start.6
  58.8 276.5 %copy-start.4 = (f32[4096]{0:T(1024)S(1)}, f32[4096]{0:T(1024)}, u32[]{:S(2)}) copy-start(f32[4096]{0:T(1024)} %param.18) | copy-start | bytes 49156
  59.4 1.3 copy-start.1
  60.8 362.2 %copy-start.8 = (bf16[2,64,4096]{2,1,0:T(8,128)(2,1)S(1)}, bf16[2,64,4096]{2,1,0:T(8,128)(2,1)}, u32[]{:S(2)}) copy-start(bf16[2,64,4096]{2,1,0:T(8,128)(2,1)} %param.21) | copy-start | bytes 3145732
  60.8 362.2 %all-gather.6.cloned.1.call-start = ((), (), s32[]{:S(2)}) async-start(), calls=%async_computation.5 | async-start | bytes 8912896 | tf_op jit(solution)/shard_map/all_gather | solution.py:113
  338.2 181.0 %all-gather.4.cloned.1.call-start = ((), (), s32[]{:S(2)}) async-start(), calls=%async_computation.3 | async-start | bytes 8912896 | tf_op jit(solution)/shard_map/all_gather | solution.py:119
  423.0 5.9 copy-start.7
  423.0 6.0 copy-start.9
  429.0 90.3 %copy-start.2 = (bf16[2,1024,256]{2,1,0:T(8,128)(2,1)S(1)}, bf16[2,1024,256]{2,1,0:T(8,128)(2,1)}, u32[]{:S(2)}) copy-start(bf16[2,1024,256]{2,1,0:T(8,128)(2,1)} %param.23) | copy-start | bytes 3145732
  432.8 99.3 %copy-start.5 = (f32[128,8]{0,1:T(8,128)S(1)}, f32[128,8]{0,1:T(8,128)}, u32[]{:S(2)}) copy-start(f32[128,8]{0,1:T(8,128)} %param.20) | copy-start | bytes 12292
  526.3 15.9 %all-to-all-start = ((bf16[16,2,32,256]{3,2,1,0:T(8,128)(2,1)}), bf16[16,2,32,256]{3,2,1,0:T(8,128)(2,1)S(1)}, u32[]{:S(2)}, u32[]{:S(2)}) async-start(bf16[16,2,32,256]{3,2,1,0:T(8,128)(2,1)} %copy.39), calls=%async_computation | async-start | bytes 1048576 | tf_op jit(solution)/shard_map/all_to_all | solution.py:123
  532.1 150.3 %reduce-scatter.2.cloned.1.call-start = ((), (), s32[]{:S(2)}) async-start(), calls=%async_computation.4 | async-start | bytes 2162688 | tf_op jit(solution)/shard_map/reduce_scatter | solution.py:130
Sparse Core Ops, SparseCore 0:
  60.9 272.5 all-reduce.1
  338.3 84.5 all-gather.5
  433.0 86.2 all-gather.3
  545.0 137.3 reduce-scatter.1
where the time goes:
time: 691 us; the launch traced here: 690 us
  waiting for transfers between devices  590 us (85%)
  blocking collectives  48.1 us (7%)
  matrix products  21.5 us (3%)
  between operations  13.9 us (2%)
    psum x1, waiting for transfers between devices, per_device(): residual_sum = lax.psum(partial_value, 'exp')  272 us
    reduce_scatter x1, waiting for transfers between devices, per_device(): lax.psum_scatter(expert_sum, 'exp', scatter_dimension=1, tiled=True)  136 us
    all_gather x1, waiting for transfers between devices, per_device(): lax.all_gather(hidden, 'seq', axis=3, tiled=True)  86.4 us
    all_gather x1, waiting for transfers between devices, per_device(): segment = lax.all_gather(chosen[None], 'seq', axis=0, tiled=True)  84.7 us
    all_gather x1, blocking collectives, per_device(): piece_values = lax.all_gather(head_values, 'seq', axis=0, tiled=True)  24.3 us
    all_gather x1, blocking collectives, per_device(): piece_keys = lax.all_gather(head_keys, 'seq', axis=0, tiled=True)  23.8 us
  transfers between devices with their start and end apart: 5, of which 5 were waited for; matrix products, arithmetic and copies ran while one was open for 0% of the time, Pallas kernels for 0%

commit v1 on v0

v1 whole, which is shorter than its diff:
```python
import jax
import jax.numpy as jnp
from jax import lax
from jax.experimental import pallas as pl
from jax.experimental.pallas import tpu as pltpu
from jax.sharding import PartitionSpec as P

MESH = pl.DeviceIdType.MESH
BF16 = jnp.bfloat16
F32 = jnp.float32
NEG_FILL = -1e30
NORM_EPS = 1e-06
D = 4096
HD = 128
ROWS = 128
NZ = 16
STEPS = 8
CAP = 32
CHUNKS = 4


def dot(a, b):
    return jnp.dot(a, b, preferred_element_type=F32)


def dot_t(a, b):
    return lax.dot_general(a, b, (((1,), (1,)), ((), ())), preferred_element_type=F32)


def remote(src, dst, send_sem, recv_sem, device):
    return pltpu.make_async_remote_copy(
        src_ref=src,
        dst_ref=dst,
        send_sem=send_sem,
        recv_sem=recv_sem,
        device_id=device,
        device_id_type=MESH,
    )


class Place:
    def __init__(self):
        self.s = lax.axis_index("seq")
        self.e = lax.axis_index("exp")
        self.yh = lax.div(self.s, 2)
        self.c = lax.rem(self.s, 2)
        self.y = lax.div(self.s, 4)
        self.h = lax.rem(self.yh, 2)
        self.z = lax.div(self.e, 2)
        self.l = lax.rem(self.e, 2)

    def seq_of(self, y, h, c):
        return (y * 2 + h) * 2 + c

    def y_step(self, k):
        return lax.rem(self.y + k + 4, 4)

    def z_step(self, k):
        return lax.rem(self.z + k + 32, NZ)

    def at_y(self, k):
        return (self.seq_of(self.y_step(k), self.h, self.c), self.e)

    def at_other_h(self):
        return (self.seq_of(self.y, 1 - self.h, self.c), self.e)

    def at_other_core(self):
        return (self.seq_of(self.y, self.h, 1 - self.c), self.e)

    def at_z(self, k):
        return (self.s, self.z_step(k) * 2 + self.l)

    def at_other_l(self):
        return (self.s, self.z * 2 + 1 - self.l)


class SeqGather:
    def __init__(self, me, buf, send, recv):
        self.me, self.buf, self.send, self.recv = me, buf, send, recv

    def part(self, j, y, h):
        return self.buf.at[j, y * 2 + h, self.me.c]

    def copy(self, j, k, ref, device):
        return remote(ref, ref, self.send.at[j, k], self.recv.at[j, k], device)

    def push(self, j, k):
        me = self.me
        if k < 3:
            ref = self.part(j, me.y, me.h)
        elif k < 5:
            ref = self.part(j, me.y, 1 - me.h)
        elif k == 5:
            ref = self.part(j, me.y_step(-1), me.h)
        elif k == 6:
            ref = self.part(j, me.y_step(1), 1 - me.h)
        else:
            ref = self.buf.at[j, :, me.c]
        if k == 0:
            device = me.at_other_h()
        elif k in (1, 3, 5):
            device = me.at_y(1)
        elif k in (2, 4, 6):
            device = me.at_y(-1)
        else:
            device = me.at_other_core()
        return self.copy(j, k, ref, device)

    def arrived(self, j, k):
        me = self.me
        ref = [
            lambda: self.part(j, me.y, 1 - me.h),
            lambda: self.part(j, me.y_step(-1), me.h),
            lambda: self.part(j, me.y_step(1), me.h),
            lambda: self.part(j, me.y_step(-1), 1 - me.h),
            lambda: self.part(j, me.y_step(1), 1 - me.h),
            lambda: self.part(j, me.y_step(2), me.h),
            lambda: self.part(j, me.y_step(2), 1 - me.h),
            lambda: self.buf.at[j, :, 1 - me.c],
        ][k]()
        self.copy(j, k, ref, me.at_other_core()).wait_recv()

    def a(self, j):
        for k in range(3):
            self.push(j, k).start()

    def b(self, j):
        self.arrived(j, 0)
        self.push(j, 3).start()
        self.push(j, 4).start()

    def c(self, j):
        self.arrived(j, 1)
        self.push(j, 5).start()
        self.arrived(j, 4)
        self.push(j, 6).start()
        self.arrived(j, 2)
        self.arrived(j, 3)

    def d(self, j):
        self.arrived(j, 5)
        self.arrived(j, 6)
        self.push(j, 7).start()

    def e(self, j):
        self.arrived(j, 7)

    def finish(self, j):
        for k in range(8):
            self.push(j, k).wait_send()


class ZRing:
    def __init__(self, me, buf, send, recv):
        self.me, self.buf, self.send, self.recv = me, buf, send, recv

    def up(self, k):
        ref = self.buf.at[self.me.z_step(1 - k)]
        return remote(ref, ref, self.send.at[0, k], self.recv.at[0, k], self.me.at_z(1))

    def down(self, k):
        ref = self.buf.at[self.me.z_step(k - 1)]
        return remote(ref, ref, self.send.at[1, k], self.recv.at[1, k], self.me.at_z(-1))

    def start(self):
        self.down(1).start()
        self.up(1).start()

    def step(self, j):
        me = self.me
        low, high = me.z_step(-j), me.z_step(j + 1)

        @pl.when(j >= 1)
        def _():
            ref = self.buf.at[low]
            remote(ref, ref, self.send.at[0, j], self.recv.at[0, j], me.at_z(1)).wait_recv()

            @pl.when(j < STEPS - 1)
            def _():
                self.up(j + 1).start()

        ref = self.buf.at[high]
        remote(ref, ref, self.send.at[1, j + 1], self.recv.at[1, j + 1], me.at_z(-1)).wait_recv()

        @pl.when(j < STEPS - 1)
        def _():
            self.down(j + 2).start()

        return low, high

    def finish(self):
        def one(k, _):
            self.down(k).wait_send()

            @pl.when(k < STEPS)
            def _():
                self.up(k).wait_send()

            return 0

        lax.fori_loop(1, STEPS + 1, one, 0)


def kernel(
    q_ref, res_ref, gain_ref, ids_ref, score_ref,
    key_hbm, val_hbm, proj_hbm, wg_hbm, wu_hbm, wd_hbm,
    attn_ref, out_ref,
    kv, strip, wp, heads, partial, partial_in, xcols, xs, sx,
    wg, wu, wd, wcat, wdz, acc, ssq, hid, prod, ret, table, spread,
    ring_in, ring_out,
    local_sem, kv_send, kv_recv, wz_send, wz_recv, wp_send, wp_recv,
    hz_send, hz_recv, pl_send, pl_recv, xz_send, xz_recv, xl_send, xl_recv,
    xs_send, xs_recv, hid_send, hid_recv, ret_send, ret_recv, rz_send, rz_recv,
):
    me = Place()
    s, z, l = me.s, me.z, me.l

    group = pl.multiple_of(lax.div(z, 4) * HD, HD)
    loads = [
        pltpu.make_async_copy(key_hbm.at[:, pl.ds(group, HD)], kv.at[0, me.yh, me.c, 0], local_sem.at[0]),
        pltpu.make_async_copy(val_hbm.at[:, pl.ds(group, HD)], kv.at[0, me.yh, me.c, 1], local_sem.at[1]),
        pltpu.make_async_copy(
            proj_hbm.at[pl.ds(pl.multiple_of(me.yh * 16, 16), 16), :], strip, local_sem.at[2]
        ),
        pltpu.make_async_copy(wg_hbm, wg, local_sem.at[3]),
        pltpu.make_async_copy(wu_hbm, wu, local_sem.at[4]),
        pltpu.make_async_copy(wd_hbm, wd, local_sem.at[5]),
    ]
    for cp in loads:
        cp.start()

    def z_peer(d):
        return (s, me.z_step(d) * 2 + l)

    def cross_peer(d):
        return (lax.rem(s + lax.div(d, 2), 16), z * 2 + lax.rem(l + d, 2))

    def seq_peer_back(d):
        return (lax.rem(s + 16 - lax.div(d, 2), 16), z * 2 + lax.rem(l + d, 2))

    barrier = pltpu.get_barrier_semaphore()

    def greet_z(d, _):
        pl.semaphore_signal(barrier, inc=1, device_id=z_peer(d), device_id_type=MESH)
        return 0

    def greet_cross(d, _):
        pl.semaphore_signal(barrier, inc=1, device_id=cross_peer(d), device_id_type=MESH)
        return 0

    lax.fori_loop(1, 32, greet_cross, 0)
    lax.fori_loop(1, NZ, greet_z, 0)
    pl.semaphore_wait(barrier, 31 + NZ - 1)

    kv_gather = SeqGather(me, kv, kv_send, kv_recv)
    wp_gather = SeqGather(me, wp, wp_send, wp_recv)
    loads[0].wait()
    loads[1].wait()
    kv_gather.a(0)
    loads[2].wait()

    def strip_copy(d):
        target = me.z_step(d)
        col = pl.multiple_of(target * 256 + me.c * HD, HD)
        return remote(
            strip.at[:, pl.ds(col, HD)],
            wp.at[0, me.yh, me.c, z],
            wz_send.at[d],
            wz_recv.at[d],
            z_peer(d),
        )

    def strip_start(d, _):
        strip_copy(d).start()
        return 0

    lax.fori_loop(1, NZ, strip_start, 0)
    wp[0, me.yh, me.c, z] = strip[:, pl.ds(pl.multiple_of(z * 256 + me.c * HD, HD), HD)]

    lane = lax.broadcasted_iota(jnp.int32, (ROWS, 128), 1)
    row = lax.broadcasted_iota(jnp.int32, (ROWS, 128), 0)
    ids = ids_ref[...]
    weight = score_ref[...] / jnp.sum(score_ref[...], axis=1, keepdims=True)
    routed = jnp.zeros((ROWS, 128), F32)
    shares = jnp.zeros((ROWS, 128), F32)
    for q in range(4):
        pair = l if q < 2 else 1 - l
        expert = 4 * z + 2 * pair + q % 2
        match = ids == expert
        lanes = lax.div(lane, CAP) == q
        routed = jnp.where(lanes, jnp.sum(jnp.where(match, 1.0, 0.0), axis=1, keepdims=True), routed)
        shares = jnp.where(lanes, jnp.sum(jnp.where(match, weight, 0.0), axis=1, keepdims=True), shares)
    earlier = jnp.where(lane < row, 1.0, 0.0).astype(BF16)
    rank = dot(earlier, routed.astype(BF16))
    chosen = (routed > 0.5) & (rank == lax.rem(lane, CAP).astype(F32))
    table[...] = jnp.where(chosen, 1.0, 0.0).T.astype(BF16)
    spread_all = jnp.where(chosen, shares, 0.0)
    spread_high = spread_all.astype(BF16)
    spread[0] = spread_high
    spread[1] = (spread_all - spread_high.astype(F32)).astype(BF16)

    kv_gather.b(0)

    def strip_wait(d, _):
        ref = wp.at[0, me.yh, me.c, me.z_step(-d)]
        remote(ref, ref, wz_send.at[d], wz_recv.at[d], z_peer(d)).wait_recv()
        return 0

    kv_gather.c(0)
    lax.fori_loop(1, NZ, strip_wait, 0)
    wp_gather.a(0)
    kv_gather.d(0)

    loads[3].wait()
    loads[4].wait()
    gain = gain_ref[...]
    zeros = jnp.zeros((64, D), BF16)
    for i in range(2):
        wcat[i, pl.ds(64 * i, 64), :] = (wg[i].astype(F32) * gain).astype(BF16)
        wcat[i, pl.ds(64 * (1 - i), 64), :] = zeros
        wcat[i, pl.ds(128 + 64 * i, 64), :] = (wu[i].astype(F32) * gain).astype(BF16)
        wcat[i, pl.ds(128 + 64 * (1 - i), 64), :] = zeros
    loads[5].wait()

    def lay_down(t, _):
        at = pl.multiple_of(t * 64, 64)
        none = jnp.zeros((64, 256), BF16)
        wdz[t, 0:64, 0:256] = wd[0, pl.ds(at, 64), :]
        wdz[t, 0:64, 256:512] = none
        wdz[t, 64:128, 0:256] = none
        wdz[t, 64:128, 256:512] = wd[1, pl.ds(at, 64), :]
        return 0

    lax.fori_loop(0, 16, lay_down, 0)
    acc[...] = jnp.zeros_like(acc)
    ssq[...] = jnp.zeros_like(ssq)
    partial[...] = jnp.zeros_like(partial)

    wp_gather.b(0)
    kv_gather.e(0)

    keys = kv[0, :, :, 0].reshape(16 * ROWS, HD)
    scores = dot_t(q_ref[...], keys) * HD ** (-0.5)
    key_pos = lax.broadcasted_iota(jnp.int32, (ROWS, 16 * ROWS), 1)
    query_pos = lax.broadcasted_iota(jnp.int32, (ROWS, 16 * ROWS), 0) + s * ROWS
    scores = jnp.where(query_pos >= key_pos, scores, NEG_FILL)
    row_max = jnp.max(scores, axis=1, keepdims=True)
    exp_weights = jnp.exp(scores - row_max)
    row_total = jnp.sum(exp_weights, axis=1, keepdims=True)
    values = kv[0, :, :, 1].reshape(16 * ROWS, HD)
    heads[z] = (dot(exp_weights.astype(BF16), values) / row_total).astype(BF16)

    head_ring = ZRing(me, heads, hz_send, hz_recv)
    head_ring.start()
    wp_gather.c(0)
    wp_gather.d(0)
    wp_gather.e(0)

    def project(j, _):
        low, high = head_ring.step(j)
        for block in (low, high):
            for half in range(2):
                columns = wp[0, :, half, block].reshape(HD, HD)
                partial[half] += dot(heads[block], columns)
        return 0

    lax.fori_loop(0, STEPS, project, 0)
    swap = remote(partial.at[1 - l], partial_in, pl_send, pl_recv, me.at_other_l())
    swap.start()
    swap.wait_recv()
    projected = partial[l] + partial_in[...]
    attn_ref[...] = projected.astype(BF16)
    xcols[z] = (projected + res_ref[...].astype(F32)).astype(BF16)

    x_ring = ZRing(me, xcols, xz_send, xz_recv)
    x_ring.start()
    xs_gather = SeqGather(me, xs, xs_send, xs_recv)

    def x_swap(j):
        return remote(
            sx.at[j],
            xs.at[j, me.yh, me.c, :, :, pl.ds(pl.multiple_of(l * HD, HD), HD)],
            xl_send.at[j],
            xl_recv.at[j],
            me.at_other_l(),
        )

    def dispatch(t, _):
        @pl.when(t < STEPS)
        def _():
            low, high = x_ring.step(t)
            for ab, block in enumerate((low, high)):
                picked = dot(table[...], xcols[block]).astype(BF16)
                xs[t, me.yh, me.c, ab, :, pl.ds(pl.multiple_of(l * HD, HD), HD)] = picked[:64]
                sx[t, ab] = picked[64:]
            x_swap(t).start()

        @pl.when((t >= 1) & (t < STEPS + 1))
        def _():
            j = t - 1
            ref = xs.at[j, me.yh, me.c, :, :, pl.ds(pl.multiple_of((1 - l) * HD, HD), HD)]
            remote(ref, ref, xl_send.at[j], xl_recv.at[j], me.at_other_l()).wait_recv()
            xs_gather.a(j)

        @pl.when((t >= 2) & (t < STEPS + 2))
        def _():
            xs_gather.b(t - 2)

        @pl.when((t >= 3) & (t < STEPS + 3))
        def _():
            xs_gather.c(t - 3)

        @pl.when((t >= 4) & (t < STEPS + 4))
        def _():
            xs_gather.d(t - 4)

        @pl.when(t >= 5)
        def _():
            j = t - 5
            xs_gather.e(j)
            for ab, block in enumerate((me.z_step(-j), me.z_step(j + 1))):
                col = pl.multiple_of(block * 256, 256)
                for i in range(2):
                    x = xs[j, :, :, ab, pl.ds(i * CAP, CAP), :].reshape(16 * CAP, 256)
                    acc[...] += dot_t(x, wcat[i, :, pl.ds(col, 256)])
                    wide = x.astype(F32)
                    square = wide * wide
                    ssq[i] += square[:, :128] + square[:, 128:]

        return 0

    lax.fori_loop(0, STEPS + 5, dispatch, 0)

    half = lax.broadcasted_iota(jnp.int32, (ROWS, 128), 1) < 64
    hid_gather = SeqGather(me, hid, hid_send, hid_recv)
    for k in range(CHUNKS):
        rows = pl.ds(k * ROWS, ROWS)
        scales = [
            lax.rsqrt(jnp.sum(ssq[i, rows, :], axis=1, keepdims=True) * (1.0 / D) + NORM_EPS)
            for i in range(2)
        ]
        scale = jnp.where(half, scales[0], scales[1])
        gate = acc[rows, 0:128] * scale
        up = acc[rows, 128:256] * scale
        hid[k, me.yh, me.c] = (gate / (1.0 + jnp.exp(-gate)) * up).astype(BF16)
        hid_gather.a(k)

    def hidden(t, _):
        @pl.when(t < CHUNKS)
        def _():
            hid_gather.b(t)

        @pl.when((t >= 1) & (t < CHUNKS + 1))
        def _():
            hid_gather.c(t - 1)

        @pl.when((t >= 2) & (t < CHUNKS + 2))
        def _():
            hid_gather.d(t - 2)

        @pl.when(t >= 3)
        def _():
            k = t - 3
            hid_gather.e(k)
            total = jnp.zeros((ROWS, 512), F32)
            for yh in range(8):
                for c in range(2):
                    total += dot(hid[k, yh, c], wdz[yh * 2 + c])
            made = total.astype(BF16)
            for i in range(2):
                prod[pl.ds(k * 4, 4), pl.ds(i * CAP, CAP), :] = made[:, i * 256:(i + 1) * 256].reshape(4, CAP, 256)

        return 0

    lax.fori_loop(0, CHUNKS + 3, hidden, 0)

    def back_copy(d):
        target_s = lax.rem(s + lax.div(d, 2), 16)
        target_l = lax.rem(l + d, 2)
        return remote(
            prod.at[target_s, :, pl.ds(pl.multiple_of(target_l * HD, HD), HD)],
            ret.at[s, pl.ds(pl.multiple_of(lax.rem(d, 2) * 64, 64), 64), :],
            ret_send.at[d],
            ret_recv.at[s, lax.rem(d, 2)],
            cross_peer(d),
        )

    def back_start(d, _):
        back_copy(d).start()
        return 0

    lax.fori_loop(1, 32, back_start, 0)
    ret[s, 0:64, :] = prod[s, :, pl.ds(pl.multiple_of(l * HD, HD), HD)]

    def back_wait(source, half):
        ref = ret.at[source, pl.ds(half * 64, 64), :]
        remote(ref, ref, ret_send.at[1], ret_recv.at[source, half], me.at_other_l()).wait_recv()

    def share_of(target):
        @pl.when(target != s)
        def _():
            back_wait(target, 0)

        back_wait(target, 1)
        returned = ret[target]
        return dot(spread[0], returned) + dot(spread[1], returned)

    def sum_up(k):
        return remote(ring_out.at[0, k], ring_in.at[0, k], rz_send.at[0, k], rz_recv.at[0, k], me.at_z(1))

    def sum_down(k):
        return remote(ring_out.at[1, k], ring_in.at[1, k], rz_send.at[1, k], rz_recv.at[1, k], me.at_z(-1))

    def reduce_up(k, _):
        share = share_of(me.z_step(8 - k))

        @pl.when(k == 0)
        def _():
            ring_out[0, 1] = share.astype(BF16)

        @pl.when(k >= 1)
        def _():
            sum_up(k).wait_recv()
            ring_out[0, k + 1] = (share + ring_in[0, k].astype(F32)).astype(BF16)

        sum_up(k + 1).start()

        @pl.when(k < 7)
        def _():
            other = share_of(me.z_step(-7 + k))

            @pl.when(k == 0)
            def _():
                ring_out[1, 1] = other.astype(BF16)

            @pl.when(k >= 1)
            def _():
                sum_down(k).wait_recv()
                ring_out[1, k + 1] = (other + ring_in[1, k].astype(F32)).astype(BF16)

            sum_down(k + 1).start()

        return 0

    lax.fori_loop(0, 8, reduce_up, 0)
    total = share_of(z)
    sum_down(7).wait_recv()
    total += ring_in[1, 7].astype(F32)
    sum_up(8).wait_recv()
    total += ring_in[0, 8].astype(F32)
    out_ref[...] = total.astype(BF16)

    kv_gather.finish(0)
    wp_gather.finish(0)
    head_ring.finish()
    x_ring.finish()
    swap.wait_send()

    def strip_sent(d, _):
        strip_copy(d).wait_send()
        return 0

    def back_sent(d, _):
        back_copy(d).wait_send()
        return 0

    def xs_sent(j, _):
        x_swap(j).wait_send()
        xs_gather.finish(j)
        return 0

    def hid_sent(j, _):
        hid_gather.finish(j)
        return 0

    def sums_sent(k, _):
        sum_up(k).wait_send()

        @pl.when(k < 8)
        def _():
            sum_down(k).wait_send()

        return 0

    lax.fori_loop(1, NZ, strip_sent, 0)
    lax.fori_loop(1, 32, back_sent, 0)
    lax.fori_loop(0, STEPS, xs_sent, 0)
    lax.fori_loop(0, CHUNKS, hid_sent, 0)
    lax.fori_loop(1, 9, sums_sent, 0)


def per_device(
    queries, key_states, value_states, residual, out_proj, norm_gain,
    expert_ids, gate_scores, w_gate, w_up, w_down,
):
    vmem = pl.BlockSpec(memory_space=pltpu.VMEM)
    anywhere = pl.BlockSpec(memory_space=pl.ANY)
    dma = pltpu.SemaphoreType.DMA
    block = jax.ShapeDtypeStruct((ROWS, HD), BF16)
    scratch = [
        pltpu.VMEM((1, 8, 2, 2, ROWS, HD), BF16),
        pltpu.VMEM((16, D), BF16),
        pltpu.VMEM((1, 8, 2, NZ, 16, HD), BF16),
        pltpu.VMEM((NZ, ROWS, HD), BF16),
        pltpu.VMEM((2, ROWS, HD), F32),
        pltpu.VMEM((ROWS, HD), F32),
        pltpu.VMEM((NZ, ROWS, HD), BF16),
        pltpu.VMEM((STEPS, 8, 2, 2, 64, 256), BF16),
        pltpu.VMEM((STEPS, 2, 64, HD), BF16),
        pltpu.VMEM((2, 64, D), BF16),
        pltpu.VMEM((2, 64, D), BF16),
        pltpu.VMEM((2, 1024, 256), BF16),
        pltpu.VMEM((2, 256, D), BF16),
        pltpu.VMEM((16, 128, 512), BF16),
        pltpu.VMEM((512, 256), F32),
        pltpu.VMEM((2, 512, 128), F32),
        pltpu.VMEM((CHUNKS, 8, 2, ROWS, 128), BF16),
        pltpu.VMEM((16, 64, 256), BF16),
        pltpu.VMEM((NZ, 128, HD), BF16),
        pltpu.VMEM((128, ROWS), BF16),
        pltpu.VMEM((2, ROWS, 128), BF16),
        pltpu.VMEM((2, 9, ROWS, HD), BF16),
        pltpu.VMEM((2, 9, ROWS, HD), BF16),
        dma((6,)),
        dma((1, 8)), dma((1, 8)),
        dma((NZ,)), dma((NZ,)),
        dma((1, 8)), dma((1, 8)),
        dma((2, 9)), dma((2, 9)),
        dma, dma,
        dma((2, 9)), dma((2, 9)),
        dma((STEPS,)), dma((STEPS,)),
        dma((STEPS, 8)), dma((STEPS, 8)),
        dma((CHUNKS, 8)), dma((CHUNKS, 8)),
        dma((32,)), dma((16, 2)),
        dma((2, 9)), dma((2, 9)),
    ]
    return pl.pallas_call(
        kernel,
        out_shape=(block, block),
        in_specs=[vmem] * 5 + [anywhere] * 6,
        out_specs=(vmem, vmem),
        scratch_shapes=scratch,
        compiler_params=pltpu.CompilerParams(
            collective_id=0, has_side_effects=True, vmem_limit_bytes=48 * 2**20
        ),
        cost_estimate=pl.CostEstimate(flops=2 * 10**9, bytes_accessed=8 * 10**6, transcendentals=10**6),
        name="layer",
    )(
        queries, residual, norm_gain.reshape(1, D), expert_ids, gate_scores,
        key_states, value_states, out_proj, w_gate, w_up, w_down,
    )


def solution(mesh):
    placed = (
        P("seq", "exp"),
        P("seq", None),
        P("seq", None),
        P("seq", "exp"),
        P("exp", None),
        P(),
        P("seq", None),
        P("seq", None),
        P("exp", "seq", None),
        P("exp", "seq", None),
        P("exp", None, "seq"),
    )
    return jax.shard_map(
        per_device,
        mesh=mesh,
        in_specs=placed,
        out_specs=(P("seq", "exp"), P("seq", "exp")),
        check_vma=False,
    )
```

time: 691 us -> 175 us (0.25)
  waiting for transfers between devices: 590 us -> 0 us
  Pallas kernels: 0 us -> 162 us
  blocking collectives: 48.1 us -> 0 us
  matrix products: 21.5 us -> 0 us
  between operations: 13.9 us -> 0.67 us
    psum x1 -> x0, waiting for transfers between devices: 272 us -> none  [per_device(): residual_sum = lax.psum(partial_value, 'exp')]
    all_gather x2 -> x0, waiting for transfers between devices: 171 us -> none  [the longest x1 86.4 us: per_device(): lax.all_gather(hidden, 'seq', axis=3, tiled=True)]
    pallas_call x0 -> x1, Pallas kernels: none -> 162 us  [per_device(): pl.pallas_call(kernel, out_shape=(block, block), in_specs=[vmem] * 5 + [a...]
    reduce_scatter x1 -> x0, waiting for transfers between devices: 136 us -> none  [per_device(): lax.psum_scatter(expert_sum, 'exp', scatter_dimension=1, tiled=True)]
    all_gather x2 -> x0, blocking collectives: 48.1 us -> none  [the longest x1 24.3 us: per_device(): piece_values = lax.all_gather(head_values, 'seq', axis=0, tiled=True)]
    dot_general x9 -> x0, matrix products: 21.5 us -> none  [the longest x1 6.21 us: per_device(): jnp.einsum('secf,efd->secd', lax.all_gather(hidden, 'seq', axis=3, tiled=...]
    all_to_all x1 -> x0, waiting for transfers between devices: 9.89 us -> none  [per_device(): lax.all_to_all(produced.astype(jnp.bfloat16), 'seq', split_axis=0, concat...]
    unnamed x20 -> x22, local copies, waits for them, and re-layouts: 1.52 us -> 10.9 us
  transfers between devices with their start and end apart: 5 -> 0, of which waited for: 5 -> 0; matrix products, arithmetic and copies ran while one was open for 0% -> 0% of each run, Pallas kernels for 0% -> 0%
where the time goes in v1:
time: 175 us; the launch traced here: 174 us
  Pallas kernels  162 us (93%)
  local copies, waits for them, and re-layouts  10.9 us (6%)
    pallas_call x1, Pallas kernels, per_device(): pl.pallas_call(kernel, out_shape=(block, block), in_specs=[vmem] * 5 + [a...  162 us
    unnamed x22, local copies, waits for them, and re-layouts  10.9 us

profile of v1, /device:TPU:24, one launch (start us, length us, event | category | flops | bytes accessed | tf_op | source)
XLA Modules:
  0.0 173.9 jit_solution(3707900836578679926)
XLA Ops:
  0.6 0.0 copy-start.4
  0.6 0.8 copy.13.ids_ref
  1.5 0.8 copy.14.score_ref
  2.2 0.0 copy-done.4
  2.3 0.0 copy-start
  2.3 1.2 copy-done
  3.5 0.0 copy-start.1
  3.5 1.2 copy-done.1
  4.7 0.0 copy-start.2
  4.7 1.2 copy-done.2
  5.9 0.0 copy-start.3
  5.9 1.2 copy-done.3
  7.2 0.0 copy-start.5
  7.2 0.9 copy-done.5
  8.1 0.0 copy-start.6
  8.1 0.8 copy-done.6
  8.8 0.0 copy-start.7
  8.8 0.8 copy-done.7
  9.6 0.0 copy-start.8
  9.6 0.7 copy-done.8
  10.3 162.3 %layer.1 = (bf16[128,128]{1,0:T(8,128)(2,1)S(1)}, bf16[128,128]{1,0:T(8,128)(2,1)S(1)}) custom-call(bf16[128,128]{1,0:T(8,128)(2,1)S(1)} %copy-done.6, bf16[128,128]{1,0:T(8,128)(2,1)S(1)} %copy-done.7, f32[1,4096]{1,0:T(1,128)S(1)} %bitcast.1, s32[128,8]{1,0:T(8,128)S(1)} %copy.13.ids_ref, f32[128,8]{1,0:T(8,128)S(1)} %copy.14.score_ref, ...), custom_call_target="tpu_custom_call" | custom-call | flops 2000000000 | bytes 8000000 | tf_op jit(solution)/shard_map/layer/pallas_call | solution.py:637
  172.6 0.6 copy.17
  173.3 0.6 copy.18
Async XLA Ops:
  0.6 1.6 copy-start.4
  2.3 1.2 copy-start
  3.5 1.2 copy-start.1
  4.7 1.2 copy-start.2
  5.9 1.2 copy-start.3
  7.2 0.9 copy-start.5
  8.1 0.8 copy-start.6
  8.8 0.8 copy-start.7
  9.6 0.7 copy-start.8

commit v2 on v0

v2 whole, which is shorter than its diff:
```python
import jax
import jax.numpy as jnp
from jax import lax
from jax.experimental import pallas as pl
from jax.experimental.pallas import tpu as pltpu
from jax.sharding import PartitionSpec as P

MESH = pl.DeviceIdType.MESH
BF16 = jnp.bfloat16
F32 = jnp.float32
NEG_FILL = -1e30
NORM_EPS = 1e-06
D = 4096
HD = 128
ROWS = 128
NZ = 16
STEPS = 8
CAP = 32
CHUNKS = 4
HALF = 64


def dot(a, b):
    return jnp.dot(a, b, preferred_element_type=F32)


def dot_t(a, b):
    return lax.dot_general(a, b, (((1,), (1,)), ((), ())), preferred_element_type=F32)


def remote(src, dst, send_sem, recv_sem, device):
    return pltpu.make_async_remote_copy(
        src_ref=src,
        dst_ref=dst,
        send_sem=send_sem,
        recv_sem=recv_sem,
        device_id=device,
        device_id_type=MESH,
    )


class Place:
    def __init__(self):
        self.s = lax.axis_index("seq")
        self.e = lax.axis_index("exp")
        self.yh = lax.div(self.s, 2)
        self.c = lax.rem(self.s, 2)
        self.y = lax.div(self.s, 4)
        self.h = lax.rem(self.yh, 2)
        self.z = lax.div(self.e, 2)
        self.l = lax.rem(self.e, 2)

    def seq_of(self, y, h, c):
        return (y * 2 + h) * 2 + c

    def y_step(self, k):
        return lax.rem(self.y + k + 4, 4)

    def z_step(self, k):
        return lax.rem(self.z + k + 32, NZ)

    def at_seq(self, yh, c):
        return (yh * 2 + c, self.e)

    def at_y(self, k):
        return (self.seq_of(self.y_step(k), self.h, self.c), self.e)

    def at_other_h(self):
        return (self.seq_of(self.y, 1 - self.h, self.c), self.e)

    def at_other_core(self):
        return (self.seq_of(self.y, self.h, 1 - self.c), self.e)

    def at_z(self, k):
        return (self.s, self.z_step(k) * 2 + self.l)

    def at_other_l(self):
        return (self.s, self.z * 2 + 1 - self.l)


class GroupGather:
    def __init__(self, me, buf, send, recv):
        self.me, self.buf, self.send, self.recv = me, buf, send, recv

    def copy(self, j, k, ref, device):
        return remote(ref, ref, self.send.at[j, k], self.recv.at[j, k], device)

    def push(self, j, k):
        me = self.me
        if k < 2:
            return self.copy(j, k, self.buf.at[j, me.y, me.c], me.at_y(1 - 2 * k))
        if k < 4:
            way = 5 - 2 * k
            return self.copy(j, k, self.buf.at[j, me.y_step(-way), me.c, k - 2], me.at_y(way))
        return self.copy(j, k, self.buf.at[j, :, me.c], me.at_other_core())

    def arrived(self, j, k):
        me = self.me
        if k < 2:
            ref = self.buf.at[j, me.y_step(2 * k - 1), me.c]
        elif k < 4:
            ref = self.buf.at[j, me.y_step(2), me.c, k - 2]
        else:
            ref = self.buf.at[j, :, 1 - me.c]
        self.copy(j, k, ref, me.at_other_core()).wait_recv()

    def a(self, j):
        self.push(j, 0).start()
        self.push(j, 1).start()

    def c(self, j):
        for k in range(2):
            self.arrived(j, k)
            self.push(j, 2 + k).start()

    def d(self, j):
        self.arrived(j, 2)
        self.arrived(j, 3)
        self.push(j, 4).start()

    def e(self, j):
        self.arrived(j, 4)

    def finish(self, j):
        for k in range(5):
            self.push(j, k).wait_send()


class ZRing:
    def __init__(self, me, buf, send, recv):
        self.me, self.buf, self.send, self.recv = me, buf, send, recv

    def piece(self, way, k, half, block):
        ref = self.buf.at[block, pl.ds(half * HALF, HALF), :]
        return remote(
            ref, ref, self.send.at[way, k, half], self.recv.at[way, k, half], self.me.at_z(1 - 2 * way)
        )

    def up(self, k, half):
        return self.piece(0, k, half, self.me.z_step(1 - k))

    def down(self, k, half):
        return self.piece(1, k, half, self.me.z_step(k - 1))

    def start(self, half):
        self.down(1, half).start()
        self.up(1, half).start()

    def step(self, j):
        low, high = self.me.z_step(-j), self.me.z_step(j + 1)
        for half in range(2):

            @pl.when(j >= 1)
            def _():
                self.piece(0, j, half, low).wait_recv()

                @pl.when(j < STEPS - 1)
                def _():
                    self.up(j + 1, half).start()

            self.piece(1, j + 1, half, high).wait_recv()

            @pl.when(j < STEPS - 1)
            def _():
                self.down(j + 2, half).start()

        return low, high

    def finish(self):
        def one(k, _):
            for half in range(2):
                self.down(k, half).wait_send()

                @pl.when(k < STEPS)
                def _():
                    self.up(k, half).wait_send()

            return 0

        lax.fori_loop(1, STEPS + 1, one, 0)


class ZSum:
    def __init__(self, me, share, inbox, outbox, send, recv):
        self.me, self.share = me, share
        self.inbox, self.outbox, self.send, self.recv = inbox, outbox, send, recv

    def copy(self, way, k, half):
        return remote(
            self.outbox.at[way, k, half],
            self.inbox.at[way, k, half],
            self.send.at[way, k, half],
            self.recv.at[way, k, half],
            self.me.at_z(1 - 2 * way),
        )

    def step(self, k, beside, first=False, last=False):
        shares = [self.share(self.me.z_step(8 - k))]
        if not last:
            shares.append(self.share(self.me.z_step(k - 7)))
        for half in range(2):
            for way, share in enumerate(shares):
                part = share[half * HALF:(half + 1) * HALF]
                if not first:
                    self.copy(way, k, half).wait_recv()
                    part = part + self.inbox[way, k, half].astype(F32)
                self.outbox[way, k + 1, half] = part.astype(BF16)
                self.copy(way, k + 1, half).start()
        beside(k)

    def run(self, beside=lambda k: None):
        self.step(0, beside, first=True)

        def one(k, _):
            self.step(k, beside)
            return 0

        lax.fori_loop(1, 7, one, 0)
        self.step(7, beside, last=True)
        own = self.share(self.me.z)
        parts = []
        for half in range(2):
            self.copy(1, 7, half).wait_recv()
            self.copy(0, 8, half).wait_recv()
            part = own[half * HALF:(half + 1) * HALF]
            parts.append(part + self.inbox[1, 7, half].astype(F32) + self.inbox[0, 8, half].astype(F32))
        return parts

    def finish(self):
        def one(k, _):
            for half in range(2):
                self.copy(0, k, half).wait_send()

                @pl.when(k < 8)
                def _():
                    self.copy(1, k, half).wait_send()

            return 0

        lax.fori_loop(1, 9, one, 0)


def kernel(
    q_hbm, res_hbm, gain_hbm, ids_hbm, score_hbm,
    key_hbm, val_hbm, proj_hbm, wg_hbm, wu_hbm, wd_hbm,
    attn_ref, out_ref,
    q_ref, res_ref, gain_ref, ids_ref, score_ref,
    kv, proj, head, partial, partial_in, xcols, xs, sx,
    wg, wu, wcat, wdown, acc, ssq, hid, prod, ret, table, spread,
    sum_in, sum_out, ring_in, ring_out,
    local_sem, kv_send, kv_recv, core_send, core_recv, wx_send, wx_recv, wy_send, wy_recv,
    ps_send, ps_recv, pl_send, pl_recv, xz_send, xz_recv, xl_send, xl_recv,
    xs_send, xs_recv, hid_send, hid_recv, ret_send, ret_recv, rz_send, rz_recv,
):
    me = Place()
    s, z, l = me.s, me.z, me.l
    block = me.y * 2 + me.c

    group = pl.multiple_of(lax.div(z, 4) * HD, HD)
    loads = [
        pltpu.make_async_copy(src, dst, local_sem.at[k])
        for k, (src, dst) in enumerate(
            [
                (key_hbm.at[:, pl.ds(group, HD)], kv.at[me.yh, me.c, 0]),
                (val_hbm.at[:, pl.ds(group, HD)], kv.at[me.yh, me.c, 1]),
                (gain_hbm, gain_ref),
                (wg_hbm, wg),
                (wu_hbm, wu),
                (q_hbm, q_ref),
                (proj_hbm, proj),
                (res_hbm, res_ref),
                (ids_hbm, ids_ref),
                (score_hbm, score_ref),
            ]
        )
    ]
    for h in range(2):
        for c in range(2):
            dst = wdown.at[:, :, c, lax.rem(me.h + h, 2), :, pl.ds(0, 256)]
            loads.append(pltpu.make_async_copy(wd_hbm.at[:, :, h, c], dst, local_sem.at[10 + 2 * h + c]))
    for cp in loads:
        cp.start()

    def seq_peer(d):
        return (lax.rem(s + d, 16), me.e)

    def group_peer(d):
        other = lax.rem(block + lax.div(d, 2), 8)
        place = me.seq_of(lax.div(other, 2), me.h, lax.rem(other, 2))
        return (place, z * 2 + lax.rem(l + d, 2))

    barrier = pltpu.get_barrier_semaphore()

    def greet_seq(d, _):
        pl.semaphore_signal(barrier, inc=1, device_id=seq_peer(d), device_id_type=MESH)
        return 0

    def greet_group(d, _):
        pl.semaphore_signal(barrier, inc=1, device_id=group_peer(2 * d + 1), device_id_type=MESH)
        return 0

    lax.fori_loop(1, 16, greet_seq, 0)
    lax.fori_loop(0, 8, greet_group, 0)
    for k in (1, -1):
        pl.semaphore_signal(barrier, inc=1, device_id=me.at_z(k), device_id_type=MESH)

    loads[2].wait()
    loads[3].wait()
    loads[4].wait()
    gain = gain_ref[...]
    for i in range(2):
        wcat[i, 0, 0:64, :] = (wg[i].astype(F32) * gain).astype(BF16)
        wcat[i, 0, 64:128, :] = (wu[i].astype(F32) * gain).astype(BF16)

    loads[0].wait()
    loads[1].wait()
    pl.semaphore_wait(barrier, 15 + 8 + 2)

    def kv_copy(d):
        ref = kv.at[me.yh, me.c]
        target = lax.rem(me.yh + d, 8)
        return remote(ref, ref, kv_send.at[d], kv_recv.at[d], me.at_seq(target, me.c))

    def kv_start(d, _):
        kv_copy(d).start()
        return 0

    lax.fori_loop(1, 8, kv_start, 0)

    for k in (8, 9):
        loads[k].wait()
    lane = lax.broadcasted_iota(jnp.int32, (128, ROWS), 1)
    slot = lax.broadcasted_iota(jnp.int32, (128, ROWS), 0)
    ids = ids_ref[...]
    weight = score_ref[...] / jnp.sum(score_ref[...], axis=0, keepdims=True)
    routed = jnp.zeros((128, ROWS), F32)
    shares = jnp.zeros((128, ROWS), F32)
    for q in range(4):
        pair = l if q < 2 else 1 - l
        match = ids == 4 * z + 2 * pair + q % 2
        here = lax.div(slot, CAP) == q
        routed = jnp.where(here, jnp.sum(jnp.where(match, 1.0, 0.0), axis=0, keepdims=True), routed)
        shares = jnp.where(here, jnp.sum(jnp.where(match, weight, 0.0), axis=0, keepdims=True), shares)
    earlier = jnp.where(slot < lane, 1.0, 0.0).astype(BF16)
    rank = dot(routed.astype(BF16), earlier)
    chosen = (routed > 0.5) & (rank == lax.rem(slot, CAP).astype(F32))
    table[...] = jnp.where(chosen, 1.0, 0.0).astype(BF16)
    spread_all = jnp.where(chosen, shares, 0.0).T
    spread_high = spread_all.astype(BF16)
    spread[0] = spread_high
    spread[1] = (spread_all - spread_high.astype(F32)).astype(BF16)
    acc[...] = jnp.zeros_like(acc)
    ssq[...] = jnp.zeros_like(ssq)
    for cp in loads[5:8] + loads[10:]:
        cp.wait()

    def kv_wait(d, _):
        ref = kv.at[lax.rem(me.yh + 8 - d, 8), me.c]
        remote(ref, ref, kv_send.at[d], kv_recv.at[d], me.at_other_core()).wait_recv()
        return 0

    lax.fori_loop(1, 8, kv_wait, 0)
    ref = kv.at[:, me.c]
    core_copy = remote(ref, ref, core_send, core_recv, me.at_other_core())
    core_copy.start()

    def weight_copy(k):
        j, ab = lax.div(k, 2), lax.rem(k, 2)
        at = me.z_step(ab * (2 * j + 1) - j)
        cols = pl.ds(pl.multiple_of(at * 256, 256), 256)
        return remote(
            wcat.at[:, 0, :, cols], wcat.at[:, 1, :, cols], wx_send.at[j, ab], wx_recv.at[j, ab], me.at_other_h()
        )

    def down_copy(h, c):
        dst = wdown.at[:, :, c, lax.rem(1 - me.h + h, 2), :, pl.ds(256, 256)]
        k = 2 * h + c
        return remote(wd_hbm.at[:, :, h, c], dst, wy_send.at[k], wy_recv.at[k], me.at_other_h())

    ref = kv.at[:, 1 - me.c]
    remote(ref, ref, core_send, core_recv, me.at_other_core()).wait_recv()

    keys = kv[:, :, 0].reshape(16 * ROWS, HD)
    scores = dot_t(q_ref[...], keys) * HD ** (-0.5)
    key_pos = lax.broadcasted_iota(jnp.int32, (ROWS, 16 * ROWS), 1)
    query_pos = lax.broadcasted_iota(jnp.int32, (ROWS, 16 * ROWS), 0) + s * ROWS
    scores = jnp.where(query_pos >= key_pos, scores, NEG_FILL)
    row_max = jnp.max(scores, axis=1, keepdims=True)
    exp_weights = jnp.exp(scores - row_max)
    row_total = jnp.sum(exp_weights, axis=1, keepdims=True)
    values = kv[:, :, 1].reshape(16 * ROWS, HD)
    head[...] = (dot(exp_weights.astype(BF16), values) / row_total).astype(BF16)

    def head_share(target):
        return dot(head[...], proj[:, pl.ds(pl.multiple_of(target * 256, 256), 256)])

    head_sum = ZSum(me, head_share, sum_in, sum_out, ps_send, ps_recv)
    x_ring = ZRing(me, xcols, xz_send, xz_recv)
    parts = head_sum.run(lambda k: weight_copy(jnp.int32(k)).start())

    def swap(half):
        return remote(
            partial.at[half, 1 - l], partial_in.at[half], pl_send.at[half], pl_recv.at[half], me.at_other_l()
        )

    for half in range(2):
        partial[half, 0] = parts[half][:, 0:HD]
        partial[half, 1] = parts[half][:, HD:]
        swap(half).start()
    for half in range(2):
        rows = pl.ds(half * HALF, HALF)
        swap(half).wait_recv()
        projected = partial[half, l] + partial_in[half]
        attn_ref[rows, :] = projected.astype(BF16)
        xcols[z, rows, :] = (projected + res_ref[rows, :].astype(F32)).astype(BF16)
        x_ring.start(half)

    xs_gather = GroupGather(me, xs, xs_send, xs_recv)

    def x_swap(j):
        return remote(
            sx.at[j],
            xs.at[j, me.y, me.c, :, :, pl.ds(pl.multiple_of(l * HD, HD), HD)],
            xl_send.at[j],
            xl_recv.at[j],
            me.at_other_l(),
        )

    def dispatch(t, _):
        @pl.when(t < STEPS)
        def _():
            low, high = x_ring.step(t)
            for ab, at in enumerate((low, high)):
                picked = dot(table[...], xcols[at]).astype(BF16)
                sx[t, ab] = picked[64:]
                xs[t, me.y, me.c, ab, :, pl.ds(pl.multiple_of(l * HD, HD), HD)] = picked[:64]
            x_swap(t).start()
            weight_copy(t + STEPS).start()

        @pl.when((t >= 1) & (t < STEPS + 1))
        def _():
            j = t - 1
            ref = xs.at[j, me.y, me.c, :, :, pl.ds(pl.multiple_of((1 - l) * HD, HD), HD)]
            remote(ref, ref, xl_send.at[j], xl_recv.at[j], me.at_other_l()).wait_recv()
            xs_gather.a(j)

        @pl.when((t >= 2) & (t < STEPS + 2))
        def _():
            xs_gather.c(t - 2)

        @pl.when((t >= 3) & (t < STEPS + 3))
        def _():
            xs_gather.d(t - 3)

        for h in range(2):
            for c in range(2):

                @pl.when(t == STEPS + 2 * h + c)
                def _():
                    down_copy(h, c).start()

        @pl.when(t >= 4)
        def _():
            j = t - 4
            xs_gather.e(j)
            for ab in range(2):
                at = me.z_step(j + 1) if ab else me.z_step(-j)
                cols = pl.ds(pl.multiple_of(at * 256, 256), 256)
                ref = wcat.at[:, 1, :, cols]
                remote(ref, ref, wx_send.at[j, ab], wx_recv.at[j, ab], me.at_other_h()).wait_recv()
                for i in range(2):
                    x = xs[j, :, :, ab, pl.ds(i * CAP, CAP), :].reshape(8 * CAP, 256)
                    for own in range(2):
                        acc[i, own] += dot_t(x, wcat[i, own, :, cols])
                    wide = x.astype(F32)
                    square = wide * wide
                    ssq[i] += square[:, :128] + square[:, 128:]

        return 0

    lax.fori_loop(0, STEPS + 4, dispatch, 0)

    hid_gather = GroupGather(me, hid, hid_send, hid_recv)
    for k in range(CHUNKS):
        i = k // 2
        rows = pl.ds((k % 2) * ROWS, ROWS)
        scale = lax.rsqrt(jnp.sum(ssq[i, rows, :], axis=1, keepdims=True) * (1.0 / D) + NORM_EPS)
        made = []
        for own in range(2):
            gate = acc[i, own, rows, 0:64] * scale
            up = acc[i, own, rows, 64:128] * scale
            made.append((gate / (1.0 + jnp.exp(-gate)) * up).astype(BF16))
        hid[k, me.y, me.c] = jnp.concatenate(made, axis=1).reshape(2, HALF, 128)
        hid_gather.a(k)

    def down_ready(h, c):
        dst = wdown.at[:, :, c, lax.rem(me.h + h, 2), :, pl.ds(256, 256)]
        k = 2 * h + c
        remote(dst, dst, wy_send.at[k], wy_recv.at[k], me.at_other_h()).wait_recv()

    def down(k):
        i = k // 2
        total = jnp.zeros((ROWS, 512), F32)
        for y in range(4):
            for c in range(2):
                total += dot(hid[k, y, c].reshape(ROWS, 128), wdown[i, y, c].reshape(128, 512))
        made = total.astype(BF16)
        blocks = pl.ds((k % 2) * 4, 4)
        for side in range(2):
            for half in range(2):
                at = side * 256 + half * HD
                prod[blocks, half, pl.ds(i * CAP, CAP), side * HD:(side + 1) * HD] = made[
                    :, at:at + HD
                ].reshape(4, CAP, HD)

    for t in range(CHUNKS + 2):
        if t < CHUNKS:
            hid_gather.c(t)
        if 1 <= t < CHUNKS + 1:
            hid_gather.d(t - 1)
        if t >= 2:
            hid_gather.e(t - 2)
            if t == 2:
                for h in range(2):
                    for c in range(2):
                        down_ready(h, c)
            down(t - 2)

    def back_copy(d):
        other = lax.rem(block + lax.div(d, 2), 8)
        odd = lax.rem(d, 2)
        return remote(
            prod.at[other, lax.rem(l + d, 2)],
            ret.at[block, pl.ds(pl.multiple_of(odd * 64, 64), 64), :],
            ret_send.at[d],
            ret_recv.at[d],
            group_peer(d),
        )

    def back_start(d, _):
        back_copy(d).start()
        return 0

    lax.fori_loop(1, 16, back_start, 0)
    ret[block, 0:64, :] = prod[block, l]

    def back_wait(d, _):
        odd = lax.rem(d, 2)
        other = lax.rem(block + 8 - lax.div(d, 2), 8)
        ref = ret.at[other, pl.ds(pl.multiple_of(odd * 64, 64), 64), :]
        remote(ref, ref, ret_send.at[d], ret_recv.at[d], me.at_other_l()).wait_recv()
        return 0

    lax.fori_loop(1, 16, back_wait, 0)

    def expert_share(target):
        at = lax.div(target, 4) * 2 + lax.rem(target, 2)
        side = lax.rem(lax.div(target, 2) + me.h, 2)
        returned = ret[at, :, pl.ds(pl.multiple_of(side * HD, HD), HD)]
        return dot(spread[0], returned) + dot(spread[1], returned)

    expert_sum = ZSum(me, expert_share, ring_in, ring_out, rz_send, rz_recv)
    parts = expert_sum.run()
    for half in range(2):
        out_ref[pl.ds(half * HALF, HALF), :] = parts[half].astype(BF16)

    core_copy.wait_send()
    head_sum.finish()
    x_ring.finish()
    expert_sum.finish()
    for half in range(2):
        swap(half).wait_send()
    for h in range(2):
        for c in range(2):
            down_copy(h, c).wait_send()

    def kv_sent(d, _):
        kv_copy(d).wait_send()
        return 0

    def back_sent(d, _):
        back_copy(d).wait_send()
        return 0

    def xs_sent(j, _):
        x_swap(j).wait_send()
        xs_gather.finish(j)
        weight_copy(2 * j).wait_send()
        weight_copy(2 * j + 1).wait_send()
        return 0

    def hid_sent(j, _):
        hid_gather.finish(j)
        return 0

    lax.fori_loop(1, 8, kv_sent, 0)
    lax.fori_loop(1, 16, back_sent, 0)
    lax.fori_loop(0, STEPS, xs_sent, 0)
    lax.fori_loop(0, CHUNKS, hid_sent, 0)


def per_device(
    queries, key_states, value_states, residual, out_proj, norm_gain,
    expert_ids, gate_scores, w_gate, w_up, w_down,
):
    vmem = pl.BlockSpec(memory_space=pltpu.VMEM)
    hbm = pl.BlockSpec(memory_space=pltpu.MemorySpace.HBM)
    dma = pltpu.SemaphoreType.DMA
    out = jax.ShapeDtypeStruct((ROWS, HD), BF16)
    scratch = [
        pltpu.VMEM((ROWS, HD), BF16),
        pltpu.VMEM((ROWS, HD), BF16),
        pltpu.VMEM((1, D), F32),
        pltpu.VMEM((8, ROWS), jnp.int32),
        pltpu.VMEM((8, ROWS), F32),
        pltpu.VMEM((8, 2, 2, ROWS, HD), BF16),
        pltpu.VMEM((HD, D), BF16),
        pltpu.VMEM((ROWS, HD), BF16),
        pltpu.VMEM((2, 2, HALF, HD), F32),
        pltpu.VMEM((2, HALF, HD), F32),
        pltpu.VMEM((NZ, ROWS, HD), BF16),
        pltpu.VMEM((STEPS, 4, 2, 2, 64, 256), BF16),
        pltpu.VMEM((STEPS, 2, 64, HD), BF16),
        pltpu.VMEM((2, 64, D), BF16),
        pltpu.VMEM((2, 64, D), BF16),
        pltpu.VMEM((2, 2, 128, D), BF16),
        pltpu.VMEM((2, 4, 2, 2, 64, 512), BF16),
        pltpu.VMEM((2, 2, 256, 128), F32),
        pltpu.VMEM((2, 256, 128), F32),
        pltpu.VMEM((CHUNKS, 4, 2, 2, HALF, 128), BF16),
        pltpu.VMEM((8, 2, 64, 256), BF16),
        pltpu.VMEM((8, 128, 256), BF16),
        pltpu.VMEM((128, ROWS), BF16),
        pltpu.VMEM((2, ROWS, 128), BF16),
        pltpu.VMEM((2, 9, 2, HALF, 256), BF16),
        pltpu.VMEM((2, 9, 2, HALF, 256), BF16),
        pltpu.VMEM((2, 9, 2, HALF, HD), BF16),
        pltpu.VMEM((2, 9, 2, HALF, HD), BF16),
        dma((14,)),
        dma((8,)), dma((8,)),
        dma, dma,
        dma((STEPS, 2)), dma((STEPS, 2)),
        dma((4,)), dma((4,)),
        dma((2, 9, 2)), dma((2, 9, 2)),
        dma((2,)), dma((2,)),
        dma((2, 9, 2)), dma((2, 9, 2)),
        dma((STEPS,)), dma((STEPS,)),
        dma((STEPS, 5)), dma((STEPS, 5)),
        dma((CHUNKS, 5)), dma((CHUNKS, 5)),
        dma((16,)), dma((16,)),
        dma((2, 9, 2)), dma((2, 9, 2)),
    ]
    return pl.pallas_call(
        kernel,
        out_shape=(out, out),
        in_specs=[hbm] * 11,
        out_specs=(vmem, vmem),
        scratch_shapes=scratch,
        compiler_params=pltpu.CompilerParams(
            collective_id=0, has_side_effects=True, vmem_limit_bytes=63 * 2**20
        ),
        cost_estimate=pl.CostEstimate(flops=2 * 10**9, bytes_accessed=8 * 10**6, transcendentals=10**6),
        name="layer",
    )(
        queries, residual, norm_gain.reshape(1, D), expert_ids.T, gate_scores.T,
        key_states, value_states, out_proj, w_gate, w_up,
        w_down.reshape(2, 4, 2, 2, 64, 256),
    )


def solution(mesh):
    placed = (
        P("seq", "exp"),
        P("seq", None),
        P("seq", None),
        P("seq", "exp"),
        P("exp", None),
        P(),
        P("seq", None),
        P("seq", None),
        P("exp", "seq", None),
        P("exp", "seq", None),
        P("exp", None, "seq"),
    )
    return jax.shard_map(
        per_device,
        mesh=mesh,
        in_specs=placed,
        out_specs=(P("seq", "exp"), P("seq", "exp")),
        check_vma=False,
    )
```

time: 691 us -> 154 us (0.22)
  waiting for transfers between devices: 590 us -> 0 us
  Pallas kernels: 0 us -> 150 us
  blocking collectives: 48.1 us -> 0 us
  matrix products: 21.5 us -> 0 us
  between operations: 13.9 us -> 0.65 us
    psum x1 -> x0, waiting for transfers between devices: 272 us -> none  [per_device(): residual_sum = lax.psum(partial_value, 'exp')]
    all_gather x2 -> x0, waiting for transfers between devices: 171 us -> none  [the longest x1 86.4 us: per_device(): lax.all_gather(hidden, 'seq', axis=3, tiled=True)]
    pallas_call x0 -> x1, Pallas kernels: none -> 150 us  [per_device(): pl.pallas_call(kernel, out_shape=(out, out), in_specs=[hbm] * 11, out_spe...]
    reduce_scatter x1 -> x0, waiting for transfers between devices: 136 us -> none  [per_device(): lax.psum_scatter(expert_sum, 'exp', scatter_dimension=1, tiled=True)]
    all_gather x2 -> x0, blocking collectives: 48.1 us -> none  [the longest x1 24.3 us: per_device(): piece_values = lax.all_gather(head_values, 'seq', axis=0, tiled=True)]
    dot_general x9 -> x0, matrix products: 21.5 us -> none  [the longest x1 6.21 us: per_device(): jnp.einsum('secf,efd->secd', lax.all_gather(hidden, 'seq', axis=3, tiled=...]
    all_to_all x1 -> x0, waiting for transfers between devices: 9.89 us -> none  [per_device(): lax.all_to_all(produced.astype(jnp.bfloat16), 'seq', split_axis=0, concat...]
  transfers between devices with their start and end apart: 5 -> 0, of which waited for: 5 -> 0; matrix products, arithmetic and copies ran while one was open for 0% -> 0% of each run, Pallas kernels for 0% -> 0%
where the time goes in v2:
time: 154 us; the launch traced here: 153 us
  Pallas kernels  150 us (97%)
  local copies, waits for them, and re-layouts  2 us (1%)
    pallas_call x1, Pallas kernels, per_device(): pl.pallas_call(kernel, out_shape=(out, out), in_specs=[hbm] * 11, out_spe...  150 us

profile of v2, /device:TPU:24, one launch (start us, length us, event | category | flops | bytes accessed | tf_op | source)
XLA Modules:
  0.0 153.0 jit_solution(16471912470638519145)
XLA Ops:
  0.6 150.4 %layer.1 = (bf16[128,128]{1,0:T(8,128)(2,1)}, bf16[128,128]{1,0:T(8,128)(2,1)}) custom-call(bf16[128,128]{1,0:T(8,128)(2,1)} %q_hbm.1, bf16[128,128]{1,0:T(8,128)(2,1)} %res_hbm.1, f32[1,4096]{1,0:T(1,128)} %bitcast.5, s32[8,128]{1,0:T(8,128)} %bitcast.6, f32[8,128]{1,0:T(8,128)} %bitcast.7, bf16[128,512]{1,0:T(8,128)(2,1)} %key_hbm.1, ...), custom_call_target="tpu_custom_call" | custom-call | flops 2000000000 | bytes 8000000 | tf_op jit(solution)/shard_map/layer/pallas_call | solution.py:653
  151.0 0.0 copy-start
  151.0 1.4 copy.15
  152.4 0.0 copy-done
  152.4 0.6 copy.16
Async XLA Ops:
  151.0 1.4 copy-start

commit v3 on v2

--- a/solution.py
+++ b/solution.py
@@ -130,54 +130,56 @@
     def __init__(self, me, buf, send, recv):
         self.me, self.buf, self.send, self.recv = me, buf, send, recv
 
-    def piece(self, way, k, half, block):
-        ref = self.buf.at[block, pl.ds(half * HALF, HALF), :]
+    def copy(self, way, k, block, hops):
+        ref = self.buf.at[block]
         return remote(
-            ref, ref, self.send.at[way, k, half], self.recv.at[way, k, half], self.me.at_z(1 - 2 * way)
+            ref, ref, self.send.at[way, k], self.recv.at[way, k], self.me.at_z(hops - 2 * way * hops)
         )
 
-    def up(self, k, half):
-        return self.piece(0, k, half, self.me.z_step(1 - k))
-
-    def down(self, k, half):
-        return self.piece(1, k, half, self.me.z_step(k - 1))
-
-    def start(self, half):
-        self.down(1, half).start()
-        self.up(1, half).start()
+    def up(self, k, hops=2):
+        return self.copy(0, k, self.me.z_step(hops - k), hops)
+
+    def down(self, k, hops=2):
+        return self.copy(1, k, self.me.z_step(k - hops), hops)
+
+    def start(self):
+        for hops in (1, 2):
+            self.down(hops, hops).start()
+            self.up(hops, hops).start()
 
     def step(self, j):
         low, high = self.me.z_step(-j), self.me.z_step(j + 1)
-        for half in range(2):
-
-            @pl.when(j >= 1)
+        self.copy(1, j + 1, high, 2).wait_recv()
+
+        @pl.when(j < STEPS - 2)
+        def _():
+            self.down(j + 3).start()
+
+        @pl.when(j >= 1)
+        def _():
+            self.copy(0, j, low, 2).wait_recv()
+
+            @pl.when(j < STEPS - 2)
             def _():
-                self.piece(0, j, half, low).wait_recv()
-
-                @pl.when(j < STEPS - 1)
-                def _():
-                    self.up(j + 1, half).start()
-
-            self.piece(1, j + 1, half, high).wait_recv()
-
-            @pl.when(j < STEPS - 1)
+                self.up(j + 2).start()
+
+        return low, high
+
+    def finish(self):
+        for hops in (1, 2):
+            self.down(hops, hops).wait_send()
+            self.up(hops, hops).wait_send()
+
+        def one(k, _):
+            self.down(k).wait_send()
+
+            @pl.when(k < STEPS)
             def _():
-                self.down(j + 2, half).start()
-
-        return low, high
-
-    def finish(self):
-        def one(k, _):
-            for half in range(2):
-                self.down(k, half).wait_send()
-
-                @pl.when(k < STEPS)
-                def _():
-                    self.up(k, half).wait_send()
+                self.up(k).wait_send()
 
             return 0
 
-        lax.fori_loop(1, STEPS + 1, one, 0)
+        lax.fori_loop(3, STEPS + 1, one, 0)
 
 
 class ZSum:
@@ -185,55 +187,53 @@
         self.me, self.share = me, share
         self.inbox, self.outbox, self.send, self.recv = inbox, outbox, send, recv
 
-    def copy(self, way, k, half):
+    def copy(self, way, k, hops=2):
         return remote(
-            self.outbox.at[way, k, half],
-            self.inbox.at[way, k, half],
-            self.send.at[way, k, half],
-            self.recv.at[way, k, half],
-            self.me.at_z(1 - 2 * way),
+            self.outbox.at[way, k],
+            self.inbox.at[way, k],
+            self.send.at[way, k],
+            self.recv.at[way, k],
+            self.me.at_z(hops - 2 * way * hops),
         )
 
-    def step(self, k, beside, first=False, last=False):
-        shares = [self.share(self.me.z_step(8 - k))]
-        if not last:
-            shares.append(self.share(self.me.z_step(k - 7)))
-        for half in range(2):
-            for way, share in enumerate(shares):
-                part = share[half * HALF:(half + 1) * HALF]
-                if not first:
-                    self.copy(way, k, half).wait_recv()
-                    part = part + self.inbox[way, k, half].astype(F32)
-                self.outbox[way, k + 1, half] = part.astype(BF16)
-                self.copy(way, k + 1, half).start()
+    def step(self, k, beside, first=False, hops=(2, 2)):
+        places = [(0, 8 - k, self.me.z_step(8 - k))]
+        if len(hops) > 1:
+            places.append((1, 7 - k, self.me.z_step(k - 7)))
+        shares = [self.share(target) for _, _, target in places]
+        for (way, far, _), part in zip(places, shares):
+            if not first:
+                self.copy(way, far + 2).wait_recv()
+                part = part + self.inbox[way, far + 2].astype(F32)
+            self.outbox[way, far] = part.astype(BF16)
+            self.copy(way, far, hops[way]).start()
         beside(k)
 
     def run(self, beside=lambda k: None):
         self.step(0, beside, first=True)
+        self.step(1, beside, first=True)
 
         def one(k, _):
             self.step(k, beside)
             return 0
 
-        lax.fori_loop(1, 7, one, 0)
-        self.step(7, beside, last=True)
-        own = self.share(self.me.z)
-        parts = []
-        for half in range(2):
-            self.copy(1, 7, half).wait_recv()
-            self.copy(0, 8, half).wait_recv()
-            part = own[half * HALF:(half + 1) * HALF]
-            parts.append(part + self.inbox[1, 7, half].astype(F32) + self.inbox[0, 8, half].astype(F32))
-        return parts
+        lax.fori_loop(2, 6, one, 0)
+        self.step(6, beside, hops=(2, 1))
+        self.step(7, beside, hops=(1,))
+        total = self.share(self.me.z)
+        for k in (2, 1):
+            for way in (1, 0):
+                self.copy(way, k).wait_recv()
+                total = total + self.inbox[way, k].astype(F32)
+        return total
 
     def finish(self):
         def one(k, _):
-            for half in range(2):
-                self.copy(0, k, half).wait_send()
-
-                @pl.when(k < 8)
-                def _():
-                    self.copy(1, k, half).wait_send()
+            self.copy(0, k).wait_send()
+
+            @pl.when(k < 8)
+            def _():
+                self.copy(1, k).wait_send()
 
             return 0
 
@@ -245,11 +245,11 @@
     key_hbm, val_hbm, proj_hbm, wg_hbm, wu_hbm, wd_hbm,
     attn_ref, out_ref,
     q_ref, res_ref, gain_ref, ids_ref, score_ref,
-    kv, proj, head, partial, partial_in, xcols, xs, sx,
+    kv, proj, staged, heads, xcols, xs, sx,
     wg, wu, wcat, wdown, acc, ssq, hid, prod, ret, table, spread,
     sum_in, sum_out, ring_in, ring_out,
     local_sem, kv_send, kv_recv, core_send, core_recv, wx_send, wx_recv, wy_send, wy_recv,
-    ps_send, ps_recv, pl_send, pl_recv, xz_send, xz_recv, xl_send, xl_recv,
+    proj_sem, pj_send, pj_recv, pc_send, pc_recv, hd_send, hd_recv, ps_send, ps_recv, xz_send, xz_recv, xl_send, xl_recv,
     xs_send, xs_recv, hid_send, hid_recv, ret_send, ret_recv, rz_send, rz_recv,
 ):
     me = Place()
@@ -266,8 +266,7 @@
                 (gain_hbm, gain_ref),
                 (wg_hbm, wg),
                 (wu_hbm, wu),
-                (q_hbm, q_ref),
-                (proj_hbm, proj),
+                (q_hbm, q_ref.at[0]),
                 (res_hbm, res_ref),
                 (ids_hbm, ids_ref),
                 (score_hbm, score_ref),
@@ -276,10 +275,34 @@
     ]
     for h in range(2):
         for c in range(2):
-            dst = wdown.at[:, :, c, lax.rem(me.h + h, 2), :, pl.ds(0, 256)]
-            loads.append(pltpu.make_async_copy(wd_hbm.at[:, :, h, c], dst, local_sem.at[10 + 2 * h + c]))
+            dst = wdown.at[0, :, :, c, lax.rem(me.h + h, 2)]
+            loads.append(pltpu.make_async_copy(wd_hbm.at[:, :, h, c], dst, local_sem.at[9 + 2 * h + c]))
     for cp in loads:
         cp.start()
+
+    def proj_cols(at, half):
+        return proj_hbm.at[:, pl.ds(pl.multiple_of(at * 256 + half * HD, HD), HD)]
+
+    def proj_load(at):
+        return pltpu.make_async_copy(
+            proj_cols(at, l), proj.at[0, lax.div(at, 2), lax.rem(at, 2)], proj_sem.at[at]
+        )
+
+    def proj_stage(k):
+        return pltpu.make_async_copy(proj_cols(2 * k + me.c, 1 - l), staged.at[k], proj_sem.at[NZ + k])
+
+    proj_copy = remote(staged, proj.at[1, :, me.c], pj_send, pj_recv, me.at_other_l())
+
+    def proj_load_start(at, _):
+        proj_load(at).start()
+        return 0
+
+    def proj_stage_start(k, _):
+        proj_stage(k).start()
+        return 0
+
+    lax.fori_loop(0, 8, proj_stage_start, 0)
+    lax.fori_loop(0, NZ, proj_load_start, 0)
 
     def seq_peer(d):
         return (lax.rem(s + d, 16), me.e)
@@ -301,33 +324,57 @@
 
     lax.fori_loop(1, 16, greet_seq, 0)
     lax.fori_loop(0, 8, greet_group, 0)
-    for k in (1, -1):
+    for k in (1, -1, 2, -2):
         pl.semaphore_signal(barrier, inc=1, device_id=me.at_z(k), device_id_type=MESH)
 
     loads[2].wait()
     loads[3].wait()
     loads[4].wait()
     gain = gain_ref[...]
-    for i in range(2):
-        wcat[i, 0, 0:64, :] = (wg[i].astype(F32) * gain).astype(BF16)
-        wcat[i, 0, 64:128, :] = (wu[i].astype(F32) * gain).astype(BF16)
+    for at in range(NZ):
+        cols = slice(at * 256, (at + 1) * 256)
+        for i in range(2):
+            wcat[at, 0, i, 0:64, :] = (wg[i, :, cols].astype(F32) * gain[:, cols]).astype(BF16)
+            wcat[at, 0, i, 64:128, :] = (wu[i, :, cols].astype(F32) * gain[:, cols]).astype(BF16)
 
     loads[0].wait()
     loads[1].wait()
-    pl.semaphore_wait(barrier, 15 + 8 + 2)
+    pl.semaphore_wait(barrier, 15 + 8 + 4)
 
     def kv_copy(d):
         ref = kv.at[me.yh, me.c]
         target = lax.rem(me.yh + d, 8)
         return remote(ref, ref, kv_send.at[d], kv_recv.at[d], me.at_seq(target, me.c))
 
+    q_copy = remote(q_hbm, q_ref.at[1], hd_send, hd_recv, me.at_other_l())
+    q_copy.start()
+
     def kv_start(d, _):
         kv_copy(d).start()
         return 0
 
     lax.fori_loop(1, 8, kv_start, 0)
 
-    for k in (8, 9):
+    def proj_staged(k, _):
+        proj_stage(k).wait()
+        return 0
+
+    lax.fori_loop(0, 8, proj_staged, 0)
+    proj_copy.start()
+    def weight_copy(k):
+        j, ab = lax.div(k, 2), lax.rem(k, 2)
+        at = me.z_step(ab * (2 * j + 1) - j)
+        return remote(
+            wcat.at[at, 0], wcat.at[at, 1], wx_send.at[j, ab], wx_recv.at[j, ab], me.at_other_h()
+        )
+
+    def down_copy(h, c):
+        dst = wdown.at[1, :, :, c, lax.rem(1 - me.h + h, 2)]
+        k = 2 * h + c
+        return remote(wd_hbm.at[:, :, h, c], dst, wy_send.at[k], wy_recv.at[k], me.at_other_h())
+
+
+    for k in (7, 8):
         loads[k].wait()
     lane = lax.broadcasted_iota(jnp.int32, (128, ROWS), 1)
     slot = lax.broadcasted_iota(jnp.int32, (128, ROWS), 0)
@@ -351,8 +398,14 @@
     spread[1] = (spread_all - spread_high.astype(F32)).astype(BF16)
     acc[...] = jnp.zeros_like(acc)
     ssq[...] = jnp.zeros_like(ssq)
-    for cp in loads[5:8] + loads[10:]:
+    for cp in loads[5:7] + loads[9:]:
         cp.wait()
+
+    def proj_loaded(at, _):
+        proj_load(at).wait()
+        return 0
+
+    lax.fori_loop(0, NZ, proj_loaded, 0)
 
     def kv_wait(d, _):
         ref = kv.at[lax.rem(me.yh + 8 - d, 8), me.c]
@@ -364,56 +417,41 @@
     core_copy = remote(ref, ref, core_send, core_recv, me.at_other_core())
     core_copy.start()
 
-    def weight_copy(k):
-        j, ab = lax.div(k, 2), lax.rem(k, 2)
-        at = me.z_step(ab * (2 * j + 1) - j)
-        cols = pl.ds(pl.multiple_of(at * 256, 256), 256)
-        return remote(
-            wcat.at[:, 0, :, cols], wcat.at[:, 1, :, cols], wx_send.at[j, ab], wx_recv.at[j, ab], me.at_other_h()
-        )
-
-    def down_copy(h, c):
-        dst = wdown.at[:, :, c, lax.rem(1 - me.h + h, 2), :, pl.ds(256, 256)]
-        k = 2 * h + c
-        return remote(wd_hbm.at[:, :, h, c], dst, wy_send.at[k], wy_recv.at[k], me.at_other_h())
-
+    proj_copy.wait_recv()
+    ref = proj.at[1, :, me.c]
+    proj_core = remote(ref, ref, pc_send, pc_recv, me.at_other_core())
+    proj_core.start()
+
+    weight_copy(jnp.int32(0)).start()
+    weight_copy(jnp.int32(1)).start()
     ref = kv.at[:, 1 - me.c]
     remote(ref, ref, core_send, core_recv, me.at_other_core()).wait_recv()
 
+    q_copy.wait_recv()
     keys = kv[:, :, 0].reshape(16 * ROWS, HD)
-    scores = dot_t(q_ref[...], keys) * HD ** (-0.5)
+    values = kv[:, :, 1].reshape(16 * ROWS, HD)
     key_pos = lax.broadcasted_iota(jnp.int32, (ROWS, 16 * ROWS), 1)
     query_pos = lax.broadcasted_iota(jnp.int32, (ROWS, 16 * ROWS), 0) + s * ROWS
-    scores = jnp.where(query_pos >= key_pos, scores, NEG_FILL)
-    row_max = jnp.max(scores, axis=1, keepdims=True)
-    exp_weights = jnp.exp(scores - row_max)
-    row_total = jnp.sum(exp_weights, axis=1, keepdims=True)
-    values = kv[:, :, 1].reshape(16 * ROWS, HD)
-    head[...] = (dot(exp_weights.astype(BF16), values) / row_total).astype(BF16)
+    for k in range(2):
+        scores = dot_t(q_ref[k], keys) * HD ** (-0.5)
+        scores = jnp.where(query_pos >= key_pos, scores, NEG_FILL)
+        row_max = jnp.max(scores, axis=1, keepdims=True)
+        exp_weights = jnp.exp(scores - row_max)
+        row_total = jnp.sum(exp_weights, axis=1, keepdims=True)
+        heads[k] = (dot(exp_weights.astype(BF16), values) / row_total).astype(BF16)
+    ref = proj.at[1, :, 1 - me.c]
+    remote(ref, ref, pc_send, pc_recv, me.at_other_core()).wait_recv()
 
     def head_share(target):
-        return dot(head[...], proj[:, pl.ds(pl.multiple_of(target * 256, 256), 256)])
+        at, odd = lax.div(target, 2), lax.rem(target, 2)
+        return dot(heads[0], proj[0, at, odd]) + dot(heads[1], proj[1, at, odd])
 
     head_sum = ZSum(me, head_share, sum_in, sum_out, ps_send, ps_recv)
+    projected = head_sum.run(lambda k: weight_copy(k + jnp.int32(2)).start())
+    attn_ref[...] = projected.astype(BF16)
+    xcols[z] = (projected + res_ref[...].astype(F32)).astype(BF16)
     x_ring = ZRing(me, xcols, xz_send, xz_recv)
-    parts = head_sum.run(lambda k: weight_copy(jnp.int32(k)).start())
-
-    def swap(half):
-        return remote(
-            partial.at[half, 1 - l], partial_in.at[half], pl_send.at[half], pl_recv.at[half], me.at_other_l()
-        )
-
-    for half in range(2):
-        partial[half, 0] = parts[half][:, 0:HD]
-        partial[half, 1] = parts[half][:, HD:]
-        swap(half).start()
-    for half in range(2):
-        rows = pl.ds(half * HALF, HALF)
-        swap(half).wait_recv()
-        projected = partial[half, l] + partial_in[half]
-        attn_ref[rows, :] = projected.astype(BF16)
-        xcols[z, rows, :] = (projected + res_ref[rows, :].astype(F32)).astype(BF16)
-        x_ring.start(half)
+    x_ring.start()
 
     xs_gather = GroupGather(me, xs, xs_send, xs_recv)
 
@@ -435,7 +473,10 @@
                 sx[t, ab] = picked[64:]
                 xs[t, me.y, me.c, ab, :, pl.ds(pl.multiple_of(l * HD, HD), HD)] = picked[:64]
             x_swap(t).start()
-            weight_copy(t + STEPS).start()
+
+            @pl.when(t < 6)
+            def _():
+                weight_copy(t + 10).start()
 
         @pl.when((t >= 1) & (t < STEPS + 1))
         def _():
@@ -455,7 +496,7 @@
         for h in range(2):
             for c in range(2):
 
-                @pl.when(t == STEPS + 2 * h + c)
+                @pl.when(t == 6 + 2 * h + c)
                 def _():
                     down_copy(h, c).start()
 
@@ -465,13 +506,12 @@
             xs_gather.e(j)
             for ab in range(2):
                 at = me.z_step(j + 1) if ab else me.z_step(-j)
-                cols = pl.ds(pl.multiple_of(at * 256, 256), 256)
-                ref = wcat.at[:, 1, :, cols]
+                ref = wcat.at[at, 1]
                 remote(ref, ref, wx_send.at[j, ab], wx_recv.at[j, ab], me.at_other_h()).wait_recv()
                 for i in range(2):
                     x = xs[j, :, :, ab, pl.ds(i * CAP, CAP), :].reshape(8 * CAP, 256)
                     for own in range(2):
-                        acc[i, own] += dot_t(x, wcat[i, own, :, cols])
+                        acc[i, own] += dot_t(x, wcat[at, own, i])
                     wide = x.astype(F32)
                     square = wide * wide
                     ssq[i] += square[:, :128] + square[:, 128:]
@@ -482,8 +522,8 @@
 
     hid_gather = GroupGather(me, hid, hid_send, hid_recv)
     for k in range(CHUNKS):
-        i = k // 2
-        rows = pl.ds((k % 2) * ROWS, ROWS)
+        i = k % 2
+        rows = pl.ds((k // 2) * ROWS, ROWS)
         scale = lax.rsqrt(jnp.sum(ssq[i, rows, :], axis=1, keepdims=True) * (1.0 / D) + NORM_EPS)
         made = []
         for own in range(2):
@@ -494,24 +534,44 @@
         hid_gather.a(k)
 
     def down_ready(h, c):
-        dst = wdown.at[:, :, c, lax.rem(me.h + h, 2), :, pl.ds(256, 256)]
+        dst = wdown.at[1, :, :, c, lax.rem(me.h + h, 2)]
         k = 2 * h + c
         remote(dst, dst, wy_send.at[k], wy_recv.at[k], me.at_other_h()).wait_recv()
 
     def down(k):
-        i = k // 2
-        total = jnp.zeros((ROWS, 512), F32)
+        i = k % 2
+        totals = [jnp.zeros((ROWS, 256), F32)] * 2
         for y in range(4):
             for c in range(2):
-                total += dot(hid[k, y, c].reshape(ROWS, 128), wdown[i, y, c].reshape(128, 512))
-        made = total.astype(BF16)
-        blocks = pl.ds((k % 2) * 4, 4)
+                rows = hid[k, y, c].reshape(ROWS, 128)
+                for side in range(2):
+                    totals[side] += dot(rows, wdown[side, i, y, c].reshape(128, 256))
+        blocks = pl.ds((k // 2) * 4, 4)
         for side in range(2):
             for half in range(2):
-                at = side * 256 + half * HD
-                prod[blocks, half, pl.ds(i * CAP, CAP), side * HD:(side + 1) * HD] = made[
-                    :, at:at + HD
-                ].reshape(4, CAP, HD)
+                made = totals[side][:, half * HD:(half + 1) * HD].astype(BF16)
+                prod[blocks, half, pl.ds(i * CAP, CAP), side * HD:(side + 1) * HD] = made.reshape(4, CAP, HD)
+
+    def back_copy(d):
+        other = lax.rem(block + lax.div(d, 2), 8)
+        odd = lax.rem(d, 2)
+        return remote(
+            prod.at[other, lax.rem(l + d, 2)],
+            ret.at[block, pl.ds(pl.multiple_of(odd * 64, 64), 64), :],
+            ret_send.at[d],
+            ret_recv.at[d],
+            group_peer(d),
+        )
+
+    def back_start(target, _):
+        for odd in range(2):
+            d = 2 * lax.rem(target + 8 - block, 8) + odd
+
+            @pl.when(d != 0)
+            def _():
+                back_copy(d).start()
+
+        return 0
 
     for t in range(CHUNKS + 2):
         if t < CHUNKS:
@@ -525,23 +585,11 @@
                     for c in range(2):
                         down_ready(h, c)
             down(t - 2)
-
-    def back_copy(d):
-        other = lax.rem(block + lax.div(d, 2), 8)
-        odd = lax.rem(d, 2)
-        return remote(
-            prod.at[other, lax.rem(l + d, 2)],
-            ret.at[block, pl.ds(pl.multiple_of(odd * 64, 64), 64), :],
-            ret_send.at[d],
-            ret_recv.at[d],
-            group_peer(d),
-        )
-
-    def back_start(d, _):
-        back_copy(d).start()
-        return 0
-
-    lax.fori_loop(1, 16, back_start, 0)
+            if t == 3:
+                lax.fori_loop(0, 4, back_start, 0)
+            if t == 5:
+                lax.fori_loop(4, 8, back_start, 0)
+
     ret[block, 0:64, :] = prod[block, l]
 
     def back_wait(d, _):
@@ -560,16 +608,14 @@
         return dot(spread[0], returned) + dot(spread[1], returned)
 
     expert_sum = ZSum(me, expert_share, ring_in, ring_out, rz_send, rz_recv)
-    parts = expert_sum.run()
-    for half in range(2):
-        out_ref[pl.ds(half * HALF, HALF), :] = parts[half].astype(BF16)
+    out_ref[...] = expert_sum.run().astype(BF16)
 
     core_copy.wait_send()
     head_sum.finish()
     x_ring.finish()
     expert_sum.finish()
-    for half in range(2):
-        swap(half).wait_send()
+    proj_core.wait_send()
+    q_copy.wait_send()
     for h in range(2):
         for c in range(2):
             down_copy(h, c).wait_send()
@@ -577,6 +623,8 @@
     def kv_sent(d, _):
         kv_copy(d).wait_send()
         return 0
+
+    proj_copy.wait_send()
 
     def back_sent(d, _):
         back_copy(d).wait_send()
@@ -608,23 +656,22 @@
     dma = pltpu.SemaphoreType.DMA
     out = jax.ShapeDtypeStruct((ROWS, HD), BF16)
     scratch = [
-        pltpu.VMEM((ROWS, HD), BF16),
+        pltpu.VMEM((2, ROWS, HD), BF16),
         pltpu.VMEM((ROWS, HD), BF16),
         pltpu.VMEM((1, D), F32),
         pltpu.VMEM((8, ROWS), jnp.int32),
         pltpu.VMEM((8, ROWS), F32),
         pltpu.VMEM((8, 2, 2, ROWS, HD), BF16),
-        pltpu.VMEM((HD, D), BF16),
-        pltpu.VMEM((ROWS, HD), BF16),
-        pltpu.VMEM((2, 2, HALF, HD), F32),
-        pltpu.VMEM((2, HALF, HD), F32),
+        pltpu.VMEM((2, 8, 2, HD, HD), BF16),
+        pltpu.VMEM((8, HD, HD), BF16),
+        pltpu.VMEM((2, ROWS, HD), BF16),
         pltpu.VMEM((NZ, ROWS, HD), BF16),
         pltpu.VMEM((STEPS, 4, 2, 2, 64, 256), BF16),
         pltpu.VMEM((STEPS, 2, 64, HD), BF16),
         pltpu.VMEM((2, 64, D), BF16),
         pltpu.VMEM((2, 64, D), BF16),
-        pltpu.VMEM((2, 2, 128, D), BF16),
-        pltpu.VMEM((2, 4, 2, 2, 64, 512), BF16),
+        pltpu.VMEM((NZ, 2, 2, 128, 256), BF16),
+        pltpu.VMEM((2, 2, 4, 2, 2, 64, 256), BF16),
         pltpu.VMEM((2, 2, 256, 128), F32),
         pltpu.VMEM((2, 256, 128), F32),
         pltpu.VMEM((CHUNKS, 4, 2, 2, HALF, 128), BF16),
@@ -632,23 +679,26 @@
         pltpu.VMEM((8, 128, 256), BF16),
         pltpu.VMEM((128, ROWS), BF16),
         pltpu.VMEM((2, ROWS, 128), BF16),
-        pltpu.VMEM((2, 9, 2, HALF, 256), BF16),
-        pltpu.VMEM((2, 9, 2, HALF, 256), BF16),
-        pltpu.VMEM((2, 9, 2, HALF, HD), BF16),
-        pltpu.VMEM((2, 9, 2, HALF, HD), BF16),
-        dma((14,)),
+        pltpu.VMEM((2, 9, ROWS, HD), BF16),
+        pltpu.VMEM((2, 9, ROWS, HD), BF16),
+        pltpu.VMEM((2, 9, ROWS, HD), BF16),
+        pltpu.VMEM((2, 9, ROWS, HD), BF16),
+        dma((13,)),
         dma((8,)), dma((8,)),
         dma, dma,
         dma((STEPS, 2)), dma((STEPS, 2)),
         dma((4,)), dma((4,)),
-        dma((2, 9, 2)), dma((2, 9, 2)),
-        dma((2,)), dma((2,)),
-        dma((2, 9, 2)), dma((2, 9, 2)),
+        dma((NZ + 8,)),
+        dma, dma,
+        dma, dma,
+        dma, dma,
+        dma((2, 9)), dma((2, 9)),
+        dma((2, 9)), dma((2, 9)),
         dma((STEPS,)), dma((STEPS,)),
         dma((STEPS, 5)), dma((STEPS, 5)),
         dma((CHUNKS, 5)), dma((CHUNKS, 5)),
         dma((16,)), dma((16,)),
-        dma((2, 9, 2)), dma((2, 9, 2)),
+        dma((2, 9)), dma((2, 9)),
     ]
     return pl.pallas_call(
         kernel,

time: 154 us -> 141 us (0.916)
  Pallas kernels: 150 us -> 138 us
    pallas_call x1, Pallas kernels: 150 us -> 138 us  [per_device(): pl.pallas_call(kernel, out_shape=(out, out), in_specs=[hbm] * 11, out_spe...]
where the time goes in v3:
time: 141 us
  Pallas kernels  138 us (98%)
  local copies, waits for them, and re-layouts  2 us (1%)
    pallas_call x1, Pallas kernels, per_device(): pl.pallas_call(kernel, out_shape=(out, out), in_specs=[hbm] * 11, out_spe...  138 us

profile of v3, /device:TPU:24, one launch (start us, length us, event | category | flops | bytes accessed | tf_op | source)
XLA Modules:
  0.0 141.0 jit_solution(3888564206436656558)
XLA Ops:
  0.6 138.4 %layer.1 = (bf16[128,128]{1,0:T(8,128)(2,1)}, bf16[128,128]{1,0:T(8,128)(2,1)}) custom-call(bf16[128,128]{1,0:T(8,128)(2,1)} %q_hbm.1, bf16[128,128]{1,0:T(8,128)(2,1)} %res_hbm.1, f32[1,4096]{1,0:T(1,128)} %bitcast.5, s32[8,128]{1,0:T(8,128)} %bitcast.6, f32[8,128]{1,0:T(8,128)} %bitcast.7, bf16[128,512]{1,0:T(8,128)(2,1)} %key_hbm.1, ...), custom_call_target="tpu_custom_call" | custom-call | flops 2000000000 | bytes 8000000 | tf_op jit(solution)/shard_map/layer/pallas_call | solution.py:703
  139.0 0.0 copy-start
  139.0 1.4 copy.15
  140.4 0.0 copy-done
  140.4 0.6 copy.16
Async XLA Ops:
  139.0 1.4 copy-start

commit v4 on v3

--- a/solution.py
+++ b/solution.py
@@ -87,42 +87,32 @@
 
     def push(self, j, k):
         me = self.me
-        if k < 2:
-            return self.copy(j, k, self.buf.at[j, me.y, me.c], me.at_y(1 - 2 * k))
-        if k < 4:
-            way = 5 - 2 * k
-            return self.copy(j, k, self.buf.at[j, me.y_step(-way), me.c, k - 2], me.at_y(way))
+        if k < 3:
+            return self.copy(j, k, self.buf.at[j, me.y, me.c], me.at_y((1, -1, 2)[k]))
         return self.copy(j, k, self.buf.at[j, :, me.c], me.at_other_core())
 
     def arrived(self, j, k):
         me = self.me
-        if k < 2:
-            ref = self.buf.at[j, me.y_step(2 * k - 1), me.c]
-        elif k < 4:
-            ref = self.buf.at[j, me.y_step(2), me.c, k - 2]
+        if k < 3:
+            ref = self.buf.at[j, me.y_step((-1, 1, 2)[k]), me.c]
         else:
             ref = self.buf.at[j, :, 1 - me.c]
         self.copy(j, k, ref, me.at_other_core()).wait_recv()
 
     def a(self, j):
-        self.push(j, 0).start()
-        self.push(j, 1).start()
-
-    def c(self, j):
-        for k in range(2):
+        for k in (2, 0, 1):
+            self.push(j, k).start()
+
+    def d(self, j):
+        for k in range(3):
             self.arrived(j, k)
-            self.push(j, 2 + k).start()
-
-    def d(self, j):
-        self.arrived(j, 2)
+        self.push(j, 3).start()
+
+    def e(self, j):
         self.arrived(j, 3)
-        self.push(j, 4).start()
-
-    def e(self, j):
-        self.arrived(j, 4)
 
     def finish(self, j):
-        for k in range(5):
+        for k in range(4):
             self.push(j, k).wait_send()
 
 
@@ -487,11 +477,7 @@
 
         @pl.when((t >= 2) & (t < STEPS + 2))
         def _():
-            xs_gather.c(t - 2)
-
-        @pl.when((t >= 3) & (t < STEPS + 3))
-        def _():
-            xs_gather.d(t - 3)
+            xs_gather.d(t - 2)
 
         for h in range(2):
             for c in range(2):
@@ -500,9 +486,9 @@
                 def _():
                     down_copy(h, c).start()
 
-        @pl.when(t >= 4)
+        @pl.when(t >= 3)
         def _():
-            j = t - 4
+            j = t - 3
             xs_gather.e(j)
             for ab in range(2):
                 at = me.z_step(j + 1) if ab else me.z_step(-j)
@@ -518,7 +504,7 @@
 
         return 0
 
-    lax.fori_loop(0, STEPS + 4, dispatch, 0)
+    lax.fori_loop(0, STEPS + 3, dispatch, 0)
 
     hid_gather = GroupGather(me, hid, hid_send, hid_recv)
     for k in range(CHUNKS):
@@ -573,21 +559,19 @@
 
         return 0
 
-    for t in range(CHUNKS + 2):
+    for t in range(CHUNKS + 1):
         if t < CHUNKS:
-            hid_gather.c(t)
-        if 1 <= t < CHUNKS + 1:
-            hid_gather.d(t - 1)
-        if t >= 2:
-            hid_gather.e(t - 2)
-            if t == 2:
+            hid_gather.d(t)
+        if t >= 1:
+            hid_gather.e(t - 1)
+            if t == 1:
                 for h in range(2):
                     for c in range(2):
                         down_ready(h, c)
-            down(t - 2)
-            if t == 3:
+            down(t - 1)
+            if t == 2:
                 lax.fori_loop(0, 4, back_start, 0)
-            if t == 5:
+            if t == 4:
                 lax.fori_loop(4, 8, back_start, 0)
 
     ret[block, 0:64, :] = prod[block, l]
@@ -695,8 +679,8 @@
         dma((2, 9)), dma((2, 9)),
         dma((2, 9)), dma((2, 9)),
         dma((STEPS,)), dma((STEPS,)),
-        dma((STEPS, 5)), dma((STEPS, 5)),
-        dma((CHUNKS, 5)), dma((CHUNKS, 5)),
+        dma((STEPS, 4)), dma((STEPS, 4)),
+        dma((CHUNKS, 4)), dma((CHUNKS, 4)),
         dma((16,)), dma((16,)),
         dma((2, 9)), dma((2, 9)),
     ]

time: 141 us -> 138 us (0.979)
  Pallas kernels: 138 us -> 135 us
    pallas_call x1, Pallas kernels: 138 us -> 135 us  [per_device(): pl.pallas_call(kernel, out_shape=(out, out), in_specs=[hbm] * 11, out_spe...]
where the time goes in v4:
time: 138 us
  Pallas kernels  135 us (98%)
  local copies, waits for them, and re-layouts  2 us (1%)
    pallas_call x1, Pallas kernels, per_device(): pl.pallas_call(kernel, out_shape=(out, out), in_specs=[hbm] * 11, out_spe...  135 us

profile of v4, /device:TPU:24, one launch (start us, length us, event | category | flops | bytes accessed | tf_op | source)
XLA Modules:
  0.0 137.9 jit_solution(12680385373115634331)
XLA Ops:
  0.6 135.2 %layer.1 = (bf16[128,128]{1,0:T(8,128)(2,1)}, bf16[128,128]{1,0:T(8,128)(2,1)}) custom-call(bf16[128,128]{1,0:T(8,128)(2,1)} %q_hbm.1, bf16[128,128]{1,0:T(8,128)(2,1)} %res_hbm.1, f32[1,4096]{1,0:T(1,128)} %bitcast.5, s32[8,128]{1,0:T(8,128)} %bitcast.6, f32[8,128]{1,0:T(8,128)} %bitcast.7, bf16[128,512]{1,0:T(8,128)(2,1)} %key_hbm.1, ...), custom_call_target="tpu_custom_call" | custom-call | flops 2000000000 | bytes 8000000 | tf_op jit(solution)/shard_map/layer/pallas_call | solution.py:687
  135.9 0.0 copy-start
  135.9 1.4 %copy.15 = bf16[128,128]{1,0:T(8,128)(2,1)} copy(bf16[128,128]{1,0:T(8,128)(2,1)} %get-tuple-element.4) | data formatting | bytes 65536
  137.3 0.0 copy-done
  137.3 0.6 copy.16
Async XLA Ops:
  135.9 1.4 %copy-start = (bf16[128,128]{1,0:T(8,128)(2,1)S(1)}, bf16[128,128]{1,0:T(8,128)(2,1)}, u32[]{:S(2)}) copy-start(bf16[128,128]{1,0:T(8,128)(2,1)} %get-tuple-element.5) | copy-start | bytes 98308

commit v5 on v4

--- a/solution.py
+++ b/solution.py
@@ -583,6 +583,36 @@
         remote(ref, ref, ret_send.at[d], ret_recv.at[d], me.at_other_l()).wait_recv()
         return 0
 
+    core_copy.wait_send()
+    head_sum.finish()
+    x_ring.finish()
+    proj_core.wait_send()
+    q_copy.wait_send()
+    for h in range(2):
+        for c in range(2):
+            down_copy(h, c).wait_send()
+
+    def kv_sent(d, _):
+        kv_copy(d).wait_send()
+        return 0
+
+    proj_copy.wait_send()
+
+    def xs_sent(j, _):
+        x_swap(j).wait_send()
+        xs_gather.finish(j)
+        weight_copy(2 * j).wait_send()
+        weight_copy(2 * j + 1).wait_send()
+        return 0
+
+    def hid_sent(j, _):
+        hid_gather.finish(j)
+        return 0
+
+    lax.fori_loop(1, 8, kv_sent, 0)
+    lax.fori_loop(0, STEPS, xs_sent, 0)
+    lax.fori_loop(0, CHUNKS, hid_sent, 0)
+
     lax.fori_loop(1, 16, back_wait, 0)
 
     def expert_share(target):
@@ -594,41 +624,13 @@
     expert_sum = ZSum(me, expert_share, ring_in, ring_out, rz_send, rz_recv)
     out_ref[...] = expert_sum.run().astype(BF16)
 
-    core_copy.wait_send()
-    head_sum.finish()
-    x_ring.finish()
     expert_sum.finish()
-    proj_core.wait_send()
-    q_copy.wait_send()
-    for h in range(2):
-        for c in range(2):
-            down_copy(h, c).wait_send()
-
-    def kv_sent(d, _):
-        kv_copy(d).wait_send()
-        return 0
-
-    proj_copy.wait_send()
 
     def back_sent(d, _):
         back_copy(d).wait_send()
         return 0
 
-    def xs_sent(j, _):
-        x_swap(j).wait_send()
-        xs_gather.finish(j)
-        weight_copy(2 * j).wait_send()
-        weight_copy(2 * j + 1).wait_send()
-        return 0
-
-    def hid_sent(j, _):
-        hid_gather.finish(j)
-        return 0
-
-    lax.fori_loop(1, 8, kv_sent, 0)
     lax.fori_loop(1, 16, back_sent, 0)
-    lax.fori_loop(0, STEPS, xs_sent, 0)
-    lax.fori_loop(0, CHUNKS, hid_sent, 0)
 
 
 def per_device(

time: 138 us -> 138 us (level)
  no operation moved by 1% of the time
where the time goes in v5:
time: 138 us
  Pallas kernels  135 us (98%)
  local copies, waits for them, and re-layouts  2 us (1%)
    pallas_call x1, Pallas kernels, per_device(): pl.pallas_call(kernel, out_shape=(out, out), in_specs=[hbm] * 11, out_spe...  135 us

profile of v5, /device:TPU:24, one launch (start us, length us, event | category | flops | bytes accessed | tf_op | source)
XLA Modules:
  0.0 137.6 jit_solution(2500785792997678985)
XLA Ops:
  0.6 134.9 %layer.1 = (bf16[128,128]{1,0:T(8,128)(2,1)}, bf16[128,128]{1,0:T(8,128)(2,1)}) custom-call(bf16[128,128]{1,0:T(8,128)(2,1)} %q_hbm.1, bf16[128,128]{1,0:T(8,128)(2,1)} %res_hbm.1, f32[1,4096]{1,0:T(1,128)} %bitcast.5, s32[8,128]{1,0:T(8,128)} %bitcast.6, f32[8,128]{1,0:T(8,128)} %bitcast.7, bf16[128,512]{1,0:T(8,128)(2,1)} %key_hbm.1, ...), custom_call_target="tpu_custom_call" | custom-call | flops 2000000000 | bytes 8000000 | tf_op jit(solution)/shard_map/layer/pallas_call | solution.py:689
  135.6 0.0 copy-start
  135.6 1.4 %copy.15 = bf16[128,128]{1,0:T(8,128)(2,1)} copy(bf16[128,128]{1,0:T(8,128)(2,1)} %get-tuple-element.4) | data formatting | bytes 65536
  136.9 0.0 copy-done
  136.9 0.6 copy.16
Async XLA Ops:
  135.6 1.4 %copy-start = (bf16[128,128]{1,0:T(8,128)(2,1)S(1)}, bf16[128,128]{1,0:T(8,128)(2,1)}, u32[]{:S(2)}) copy-start(bf16[128,128]{1,0:T(8,128)(2,1)} %get-tuple-element.5) | copy-start | bytes 98308
